TPU v7x, 128 devices: a whole 4x4x4 slice. The times are simulated.
128 devices in a mesh: gx: 8 (over x_lo, y), gy: 4 (over x_hi, core), gz: 4 (over z).
Axes of the slice: x: 4 (x_hi: 2, x_lo: 2; x = x_hi * 2 + x_lo), y: 4, z: 4, core: 2. Of those that a mesh axis runs over, the one named last changes fastest.
Arguments:
- hidden_in: bfloat16 [1024, 16384], P(('gy', 'gz'), 'gx'), may hold values from -8 to 8
- norm_gain: bfloat16 [16384], P('gx'), may hold values from 0.099609375 to 1.8984375
- segment_ids: int32 [1024], replicated, may hold values from 0 to 7, never falling along the last dimension, each value on 1 to 256 neighbouring positions
- query_codes: bfloat16 [16384, 16384], P('gx', ('gy', 'gz')), may hold values from -32 to 32
- query_exponents: int32 [128, 256], P('gx', ('gy', 'gz')), may hold values from -1 to 1
- key_codes: bfloat16 [16384, 2, 1024], P('gx', None, ('gy', 'gz')), may hold values from -32 to 32
- key_exponents: int32 [128, 2, 16], P('gx', None, ('gy', 'gz')), may hold values from -1 to 1
- output_codes: bfloat16 [16384, 16384], P(('gy', 'gz'), 'gx'), may hold values from -4 to 4
- output_exponents: int32 [128, 256], P(('gy', 'gz'), 'gx'), may hold values from -1 to 1
Outputs:
- layer_out: bfloat16 [1024, 16384], P(('gy', 'gz'), 'gx')
All inputs are finite; a program needn't handle non-finite values.
Results may differ from a plain program's by a relative error of at most 0.038.
Values may be sent and summed in bfloat16 or wider, within the bound.
A program may use at most 64 MiB of HBM per device.

v0:
```python
import math

import jax
import jax.numpy as jnp
from jax import lax
from jax.sharding import PartitionSpec as P

D = 16384
H = 128
HD = 128


THETA = 500000.0
EPS = 1e-05


def partner(shard, axis, distance):
    return lax.ppermute(shard, axis, [(i, i ^ 1 << distance) for i in range(lax.axis_size(axis))])


def dequant_matrix(codes, exponents, fan_in):
    rows_all, cols_all = codes.shape
    row_blocks, col_blocks = exponents.shape
    scaled = codes.astype(jnp.float32).reshape(
        row_blocks, rows_all // row_blocks, col_blocks, cols_all // col_blocks
    )
    scaled = scaled * jnp.exp2(exponents.astype(jnp.float32))[:, None, :, None]
    return (scaled.reshape(rows_all, cols_all) * (1.0 / math.sqrt(fan_in))).astype(jnp.bfloat16)


def dequant_pairs(codes, exponents, fan_in):
    rows_all, pairs, cols_all = codes.shape
    row_blocks, pairs_too, col_blocks = exponents.shape
    scaled = codes.astype(jnp.float32).reshape(
        row_blocks, rows_all // row_blocks, pairs, col_blocks, cols_all // col_blocks
    )
    scaled = scaled * jnp.exp2(exponents.astype(jnp.float32))[:, None, :, :, None]
    return (scaled.reshape(rows_all, pairs, cols_all) * (1.0 / math.sqrt(fan_in))).astype(
        jnp.bfloat16
    )


def doc_positions(segments):
    count_all = segments.shape[0]
    token_index = jnp.arange(count_all, dtype=jnp.int32)
    begins = jnp.concatenate([jnp.ones((1,), dtype=bool), segments[1:] != segments[:-1]])
    first_index = lax.cummax(jnp.where(begins, token_index, jnp.zeros_like(token_index)), axis=0)
    return token_index - first_index


def rope_tables(positions, half_size):
    exponent = jnp.arange(half_size, dtype=jnp.float32) * (-2.0 * math.log(THETA) / HD)
    frequency = jnp.exp(exponent)
    angles = positions.astype(jnp.float32)[:, None] * frequency[None, :]
    return (jnp.cos(angles), jnp.sin(angles))


def rotate(field, cosine, sine):
    half_size = field.shape[-1] // 2
    first_half = field[..., :half_size]
    second_half = field[..., half_size:]
    return jnp.concatenate(
        [first_half * cosine - second_half * sine, second_half * cosine + first_half * sine],
        axis=-1,
    )


def attend(queries, query_segments, query_index, keys, values, key_segments, key_index):
    scores = jnp.einsum("qhd,kd->hqk", queries, keys, preferred_element_type=jnp.float32) * (
        1.0 / math.sqrt(HD)
    )
    allowed = (query_segments[:, None] == key_segments[None, :]) & (
        key_index[None, :] <= query_index[:, None]
    )
    scores = jnp.where(allowed[None, :, :], scores, -jnp.inf)
    highest = jnp.max(scores, axis=2, keepdims=True)
    weights = jnp.exp(scores - highest)
    weights = (weights / jnp.sum(weights, axis=2, keepdims=True)).astype(jnp.bfloat16)
    return jnp.einsum("hqk,kd->qhd", weights, values, preferred_element_type=jnp.float32).astype(
        jnp.bfloat16
    )


def join_halves(mine, other):
    is_even = lax.axis_index("gz") % 2 == 0
    first_half = jnp.where(is_even, mine, other)
    second_half = jnp.where(is_even, other, mine)
    return jnp.concatenate([first_half, second_half], axis=-1)


def shards(
    hidden_in,
    norm_gain,
    segment_ids,
    query_codes,
    query_exponents,
    key_codes,
    key_exponents,
    output_codes,
    output_exponents,
):
    widened = hidden_in.astype(jnp.float32)
    partial_squares = jnp.sum(widened * widened, axis=1)
    squares = lax.psum(partial_squares, "gx")
    normed = (
        widened * lax.rsqrt(squares / D + EPS)[:, None] * norm_gain.astype(jnp.float32)[None, :]
    ).astype(jnp.bfloat16)
    everyone = lax.all_gather(normed, ("gy", "gz"), axis=0, tiled=True)
    tokens_all = everyone.shape[0]
    query_weight = dequant_matrix(query_codes, query_exponents, D)
    query_part = jnp.dot(everyone, query_weight, preferred_element_type=jnp.float32)
    key_weight = dequant_pairs(key_codes, key_exponents, D)
    in_rows = key_weight.shape[0]
    span = key_weight.shape[2]
    key_part = jnp.dot(
        everyone, key_weight.reshape(in_rows, 2 * span), preferred_element_type=jnp.float32
    )
    key_part = key_part.reshape(tokens_all, 2, span)
    key_value = lax.psum(key_part.astype(jnp.bfloat16), "gx")
    key_value = join_halves(key_value, partner(key_value, "gz", 0))
    positions = doc_positions(segment_ids)
    cosine, sine = rope_tables(positions, HD // 2)
    keys = rotate(key_value[:, 0].astype(jnp.float32), cosine, sine).astype(jnp.bfloat16)
    values = key_value[:, 1]
    token_index = jnp.arange(tokens_all, dtype=jnp.int32)
    heads_here = query_part.shape[1] // HD
    query_part = query_part.reshape(tokens_all, heads_here, HD)
    own_queries = lax.psum_scatter(
        query_part.astype(jnp.bfloat16), "gx", scatter_dimension=0, tiled=True
    ).astype(jnp.float32)
    block = own_queries.shape[0]
    first_row = lax.axis_index("gx") * block
    block_cosine = lax.dynamic_slice_in_dim(cosine, first_row, block, 0)
    block_sine = lax.dynamic_slice_in_dim(sine, first_row, block, 0)
    queries = rotate(own_queries, block_cosine[:, None, :], block_sine[:, None, :]).astype(
        jnp.bfloat16
    )
    block_segments = lax.dynamic_slice_in_dim(segment_ids, first_row, block, 0)
    block_index = first_row + jnp.arange(block, dtype=jnp.int32)
    attended = attend(queries, block_segments, block_index, keys, values, segment_ids, token_index)
    gathered = lax.all_gather(attended, "gx", axis=0, tiled=True)
    gathered = gathered.reshape(tokens_all, heads_here * HD)
    output_weight = dequant_matrix(output_codes, output_exponents, H * HD)
    mixed = lax.psum_scatter(
        jnp.dot(gathered, output_weight, preferred_element_type=jnp.float32).astype(jnp.bfloat16),
        ("gy", "gz"),
        scatter_dimension=0,
        tiled=True,
    ).astype(jnp.float32)
    return (widened + mixed).astype(jnp.bfloat16)


def solution(mesh):
    placed = (
        P(("gy", "gz"), "gx"),
        P("gx"),
        P(),
        P("gx", ("gy", "gz")),
        P("gx", ("gy", "gz")),
        P("gx", None, ("gy", "gz")),
        P("gx", None, ("gy", "gz")),
        P(("gy", "gz"), "gx"),
        P(("gy", "gz"), "gx"),
    )
    return jax.shard_map(
        shards, mesh=mesh, in_specs=placed, out_specs=P(("gy", "gz"), "gx"), check_vma=False
    )
```

profile of v0, /device:TPU:1, one launch (start us, length us, event | category | flops | bytes accessed | tf_op | source)
XLA Modules:
  0.0 357.3 jit_solution(11549827443247268059)
XLA Ops:
  6.5 0.7 convert_element_type.79
  7.2 1.1 fusion.28
  8.3 17.0 %psum.14 = f32[64]{0:T(128)S(1)} all-reduce(f32[64]{0:T(128)S(1)} %fusion.28), channel_id=1, replica_groups=mesh['gx'=8,'gy'=4,'gz'=4] {'gx'}, use_global_device_ids=true, to_apply=%region_1.0 | all-reduce | flops 64 | bytes 512 | tf_op jit(solution)/shard_map/psum | solution.py:104
  25.3 1.8 fusion.30
  27.2 0.7 multiply_exponential_fusion.2
  27.9 0.7 multiply_exponential_fusion
  28.7 6.5 %copy.15 = bf16[2048,1024]{0,1:T(8,128)(2,1)} copy(bf16[2048,1024]{1,0:T(8,128)(2,1)} %param.12) | data formatting | bytes 8388608 | tf_op args[3]
  35.2 0.6 mul.173
  35.9 1.6 copy-done
  37.4 6.2 %fusion.4 = bf16[2048,1024]{0,1:T(8,128)(2,1)} fusion(f32[128,8,16,128]{3,2,1,0:T(8,128)S(1)} %bitcast.95, bf16[2048,1024]{0,1:T(8,128)(2,1)S(1)} %copy-done), kind=kLoop, calls=%fused_computation.6 | loop fusion | flops 8388608 | bytes 16777216 | tf_op jit(solution)/shard_map/convert_element_type | solution.py:28
  43.7 42.7 %all-gather.3.cloned.1.call-done = bf16[1024,2048]{1,0:T(8,128)(2,1)} async-done(((bf16[64,2048]{1,0:T(8,128)(2,1)}), bf16[1024,2048]{1,0:T(8,128)(2,1)}) %all-gather.3.cloned.1.call-update) | async-done | bytes 4194320 | tf_op jit(solution)/shard_map/all_gather | solution.py:108
  86.3 4.4 %fusion.24 = bf16[1024,2,64]{0,2,1:T(8,128)(2,1)} fusion(bf16[1024,2048]{1,0:T(8,128)(2,1)} %all-gather.3.cloned.1.call-done, bf16[2048,2,64]{0,2,1:T(8,128)(2,1)S(1)} %copy-done.6, f32[2048,2]{0,1:T(2,128)S(1)} %bitcast.98), kind=kOutput, calls=%fused_computation.24 | convolution fusion | flops 538050560 | bytes 4997120 | tf_op jit(solution)/shard_map/dot_general | solution.py:115
  90.8 8.6 %fusion.20 = bf16[1024,8,128]{2,0,1:T(8,128)(2,1)} fusion(bf16[8,128,2048]{2,1,0:T(8,128)(2,1)} %bitcast.97, bf16[1024,2048]{1,0:T(8,128)(2,1)} %all-gather.3.cloned.1.call-done), kind=kOutput, calls=%fused_computation.22 | convolution fusion | flops 4296015872 | bytes 10485760 | tf_op jit(solution)/shard_map/dot_general | solution.py:111
  99.7 0.3 reduce-window.9
  100.3 56.9 %all-reduce.2.cloned.1.call-done = bf16[1024,2,64]{0,2,1:T(8,128)(2,1)} async-done(((bf16[1024,2,64]{0,2,1:T(8,128)(2,1)}), bf16[1024,2,64]{0,2,1:T(8,128)(2,1)}) %all-reduce.2.cloned.1.call-update) | async-done | bytes 262160 | tf_op jit(solution)/shard_map/psum | solution.py:119
  157.2 1.3 collective-permute-start
  158.8 3.9 %collective-permute-done = bf16[1024,2,64]{0,2,1:T(8,128)(2,1)S(1)} collective-permute-done((bf16[1024,2,64]{0,2,1:T(8,128)(2,1)}, bf16[1024,2,64]{0,2,1:T(8,128)(2,1)S(1)}, u32[]{:S(2)}, u32[]{:S(2)}) %collective-permute-start) | collective-permute-done | bytes 262176 | tf_op jit(solution)/shard_map/ppermute | solution.py:18
  162.6 1.0 broadcast_select_fusion.1
  163.7 1.2 multiply_cosine_fusion
  165.1 36.6 %reduce-scatter.3.cloned.1.call-done = bf16[128,8,128]{2,0,1:T(8,128)(2,1)} async-done(((bf16[1024,8,128]{2,0,1:T(8,128)(2,1)}), bf16[128,8,128]{2,0,1:T(8,128)(2,1)}) %reduce-scatter.3.cloned.1.call-update) | async-done | bytes 262160 | tf_op jit(solution)/shard_map/reduce_scatter | solution.py:128
  201.7 1.0 convert_element_type.92
  202.7 0.3 subtract_convert_fusion
  202.9 3.4 fusion.55
  206.3 3.4 fusion.27
  209.9 6.4 %copy.21 = bf16[1024,2048]{0,1:T(8,128)(2,1)} copy(bf16[1024,2048]{1,0:T(8,128)(2,1)} %param.16) | data formatting | bytes 8388608 | tf_op args[7]
  216.3 38.5 %all-gather.5.cloned.1.call-done = bf16[1024,8,128]{0,2,1:T(8,128)(2,1)} async-done(((bf16[128,8,128]{0,2,1:T(8,128)(2,1)}), bf16[1024,8,128]{0,2,1:T(8,128)(2,1)}) %all-gather.5.cloned.1.call-update) | async-done | bytes 2097168 | tf_op jit(solution)/shard_map/all_gather | solution.py:141
  254.7 0.6 mul.187
  255.3 1.6 copy-done.1
  256.9 0.7 copy-done.5
  257.6 6.5 %fusion.12 = bf16[1024,2048]{1,0:T(8,128)(2,1)} fusion(bf16[1024,1024]{0,1:T(8,128)(2,1)S(1)} %bitcast.100, f32[256,8,8,128]{3,2,1,0:T(8,128)S(1)} %bitcast.96, bf16[1024,2048]{0,1:T(8,128)(2,1)S(1)} %copy-done.1), kind=kOutput, calls=%fused_computation.16 | convolution fusion | flops 4305453056 | bytes 18874368 | tf_op jit(solution)/shard_map/dot_general | solution.py:145
  264.1 85.0 %reduce-scatter.5.cloned.1.call-done = bf16[64,2048]{1,0:T(8,128)(2,1)} async-done(((bf16[1024,2048]{1,0:T(8,128)(2,1)}), bf16[64,2048]{1,0:T(8,128)(2,1)}) %reduce-scatter.5.cloned.1.call-update) | async-done | bytes 262160 | tf_op jit(solution)/shard_map/reduce_scatter | solution.py:144
  349.1 1.7 fusion.31
  (41 shorter events, 1.5 us)
Async XLA Ops:
  6.5 79.8 %all-gather.3.cloned.1.call-start = ((), (), s32[]{:S(2)}) async-start(), calls=%async_computation.2 | async-start | bytes 4456448 | tf_op jit(solution)/shard_map/all_gather | solution.py:108
  27.1 130.1 %all-reduce.2.cloned.1.call-start = ((), (), s32[]{:S(2)}) async-start(), calls=%async_computation.3 | async-start | bytes 524288 | tf_op jit(solution)/shard_map/psum | solution.py:119
  35.2 2.2 copy-start
  37.4 48.9 %copy-start.6 = (bf16[2048,2,64]{0,2,1:T(8,128)(2,1)S(1)}, bf16[2048,2,64]{0,2,1:T(8,128)(2,1)}, u32[]{:S(2)}) copy-start(bf16[2048,2,64]{0,2,1:T(8,128)(2,1)} %param.14) | copy-start | bytes 1572868
  90.8 110.9 %reduce-scatter.3.cloned.1.call-start = ((), (), s32[]{:S(2)}) async-start(), calls=%async_computation.4 | async-start | bytes 2359296 | tf_op jit(solution)/shard_map/reduce_scatter | solution.py:128
  90.8 8.7 %copy-start.3 = (s32[1024]{0:T(1024)S(1)}, s32[1024]{0:T(1024)}, u32[]{:S(2)}) copy-start(s32[1024]{0:T(1024)} %param.11) | copy-start | bytes 12292
  99.4 155.3 %all-gather.5.cloned.1.call-start = ((), (), s32[]{:S(2)}) async-start(), calls=%async_computation.5 | async-start | bytes 2359296 | tf_op jit(solution)/shard_map/all_gather | solution.py:141
  157.2 5.4 %collective-permute-start = (bf16[1024,2,64]{0,2,1:T(8,128)(2,1)}, bf16[1024,2,64]{0,2,1:T(8,128)(2,1)S(1)}, u32[]{:S(2)}, u32[]{:S(2)}) collective-permute-start(bf16[1024,2,64]{0,2,1:T(8,128)(2,1)} %all-reduce.2.cloned.1.call-done), channel_id=1, source_target_pairs={{0,1},{1,0},{2,3},{3,2},{4,5},{5,4},{6,7},{7,6},{8,9},{9,8},{10,11... | collective-permute-start | bytes 786440 | tf_op jit(solution)/shard_map/ppermute | solution.py:18
  206.3 3.4 copy-start.4
  209.7 139.4 %reduce-scatter.5.cloned.1.call-start = ((), (), s32[]{:S(2)}) async-start(), calls=%async_computation.6 | async-start | bytes 4456448 | tf_op jit(solution)/shard_map/reduce_scatter | solution.py:144
  254.7 2.2 copy-start.1
  254.7 2.9 copy-start.5
  264.1 85.0 %copy-start.2 = (bf16[64,2048]{1,0:T(8,128)(2,1)S(1)}, bf16[64,2048]{1,0:T(8,128)(2,1)}, u32[]{:S(2)}) copy-start(bf16[64,2048]{1,0:T(8,128)(2,1)} %param.9) | copy-start | bytes 786436
Sparse Core Ops, SparseCore 0:
  27.2 59.0 all-gather.2
  90.9 66.2 all-reduce.1
  159.7 41.9 reduce-scatter.2
  209.8 44.8 all-gather.4
  264.2 84.8 reduce-scatter.4
where the time goes:
time: 359 us; the launch traced here: 357 us
  waiting for transfers between devices  264 us (74%)
  matrix products  26.2 us (7%)
  local copies, waits for them, and re-layouts  18.7 us (5%)
  other arithmetic  17.1 us (5%)
  blocking collectives  17 us (5%)
  between operations  13.3 us (4%)
    reduce_scatter x1, waiting for transfers between devices, shards(): lax.psum_scatter(jnp.dot(gathered, output_weight, preferred_element_type=...  85 us
    psum x1, waiting for transfers between devices, shards(): key_value = lax.psum(key_part.astype(jnp.bfloat16), 'gx')  56.9 us
    all_gather x1, waiting for transfers between devices, shards(): everyone = lax.all_gather(normed, ('gy', 'gz'), axis=0, tiled=True)  42.7 us
    all_gather x1, waiting for transfers between devices, shards(): gathered = lax.all_gather(attended, 'gx', axis=0, tiled=True)  38.5 us
    reduce_scatter x1, waiting for transfers between devices, shards(): lax.psum_scatter(query_part.astype(jnp.bfloat16), 'gx', scatter_dimension...  36.6 us
    psum x1, blocking collectives, shards(): squares = lax.psum(partial_squares, 'gx')  17 us
    unnamed x18, local copies, waits for them, and re-layouts  16.9 us
    dot_general x1, matrix products, shards(): jnp.dot(everyone, query_weight, preferred_element_type=jnp.float32)  8.56 us
  transfers between devices with their start and end apart: 6, of which 6 were waited for; matrix products, arithmetic and copies ran while one was open for 9% of the time, Pallas kernels for 0%

commit v1 on v0

v1 whole, which is shorter than its diff:
```python
import math

import jax
import jax.numpy as jnp
import numpy as np
from jax import lax
from jax.experimental import pallas as pl
from jax.experimental.pallas import tpu as pltpu
from jax.sharding import PartitionSpec as P

D = 16384
HD = 128
TOKENS = 1024
THETA = 500000.0
EPS = 1e-05
NC = 4
FEAT = 2048
QC = 1024
QW = QC + 128
F32, BF16 = jnp.float32, jnp.bfloat16
MESH = pl.DeviceIdType.MESH

A_TYPES = ["a_x", "a_zp", "a_zm", "a_s", "a_xzp", "a_xzm", "a_xs", "a_rp", "a_rm", "a_sm", "a_sp", "a_s2"]
B_TYPES = ["b_2p", "b_1p", "b_2m", "b_1m", "b_sp", "b_sm", "b_x"]
C_TYPES = ["c_x", "c_yp", "c_ym", "c_xyp", "c_xym", "c_rp", "c_rm"]
D_TYPES = ["d_s", "d_2p", "d_1p", "d_2m", "d_1m", "d_sp", "d_sm", "d_x"]
TYPES = {name: i for i, name in enumerate(A_TYPES + B_TYPES + C_TYPES + D_TYPES)}

FIRST = (
    ("A0", 0), ("A0", 1), ("DQ", 0), ("A1", 0), ("A2", 0), ("A1", 1), ("A0", 2), ("A3", 0), ("A2", 1), ("MM", 0),
    ("A1", 2), ("A0", 3), ("A3", 1), ("A2", 2), ("B2", 0), ("MM", 1), ("A1", 3), ("A3", 2), ("B3", 0), ("B2", 1),
    ("A2", 3), ("MM", 2), ("B4", 0), ("A3", 3), ("B3", 1), ("B2", 2), ("MM", 3), ("SS", 0), ("B4", 1), ("B3", 2),
    ("B2", 3), ("B4", 2), ("DO", 0), ("B3", 3), ("B4", 3),
)
SECOND = (
    ("C0", 0), ("C0", 1), ("C1", 0), ("C2", 0), ("C1", 1), ("C0", 2), ("C3", 0), ("C2", 1), ("MO", 0), ("C1", 2),
    ("C0", 3), ("C3", 1), ("C2", 2), ("D1", 0), ("MO", 1), ("C1", 3), ("C3", 2), ("D2", 0), ("D1", 1), ("C2", 3),
    ("MO", 2), ("D3", 0), ("C3", 3), ("D2", 1), ("D1", 2), ("MO", 3), ("D4", 0), ("D3", 1), ("D2", 2), ("D1", 3),
    ("D4", 1), ("D3", 2), ("D2", 3), ("D4", 2), ("D3", 3), ("D4", 3),
)


def rope_tables():
    frequency = np.exp(np.arange(HD // 2, dtype=np.float64) * (-2.0 * math.log(THETA) / HD))
    angles = np.arange(TOKENS, dtype=np.float64)[:, None] * frequency[None, :]
    cosine, sine = np.cos(angles), np.sin(angles)
    cosine = np.concatenate([cosine, cosine], axis=1).astype(np.float32)
    sine = np.concatenate([-sine, sine], axis=1).astype(np.float32)
    return cosine.reshape(8, 128, HD), sine.reshape(8, 128, HD)


def layer(
    hid, gain, segs, qc, qe, kc, ke, oc, oe, cos_hbm, sin_hbm, out,
    wq, wk, wo, kct, scale_q, scale_o, cos, sin,
    g, x, squares, sums, sums_in,
    qp, b2, bu, b3, bx, b4, qown,
    kv, kb, vb, qr,
    ag, pp, d_in, dt, d2, du, d3, dx, d4, down,
    send_sem, recv_sem, s_send, s_recv, k_send, k_recv, local,
):
    gx, gy, gz = lax.axis_index("gx"), lax.axis_index("gy"), lax.axis_index("gz")
    xlo, y, xhi, core, z = gx // 4, gx % 4, gy // 2, gy % 2, gz
    yp, ym, y2 = (y + 1) % 4, (y + 3) % 4, (y + 2) % 4
    zp, zm, z2 = (z + 1) % 4, (z + 3) % 4, (z + 2) % 4
    oxlo, oxhi, ocore = 1 - xlo, 1 - xhi, 1 - core
    odd = z % 2
    zo = z + 1 - 2 * odd
    dev_s = (gx, xhi * 2 + ocore, gz)
    dev_xhi = (gx, oxhi * 2 + core, gz)
    dev_zp, dev_zm = (gx, gy, zp), (gx, gy, zm)
    dev_xlo = (oxlo * 4 + y, gy, gz)
    dev_yp, dev_ym = (xlo * 4 + yp, gy, gz), (xlo * 4 + ym, gy, gz)
    peers = [(a, b) for a in range(2) for b in range(4) if (a, b) != (0, 0)]
    dev_peers = [(((xlo + a) % 2) * 4 + (y + b) % 4, gy, gz) for a, b in peers]
    dev_kv = [(0, 1, (gx, gy, zo))]
    for d in (1, 2):
        dev_kv += [(d, 0, ((gx + d) % 8, gy, z)), (d, 1, ((gx + d) % 8, gy, zo))]

    copies = {}

    def fetch(name, index, src, dst):
        copies[name] = pltpu.make_async_copy(src, dst, local.at[index])
        copies[name].start()

    for c in range(NC):
        fetch("hid%d" % c, c, hid.at[pl.ds(16 * c, 16), :], g.at[c, xhi, core, z])
    fetch("kc", 4, kc, kct)
    fetch("qc", 5, qc, wq)
    for d in range(3):
        fetch("cos%d" % d, 6 + d, cos_hbm.at[(gx + 8 - d) % 8], cos.at[d])
        fetch("sin%d" % d, 9 + d, sin_hbm.at[(gx + 8 - d) % 8], sin.at[d])
    fetch("oc", 12, oc, wo)

    barrier = pltpu.get_barrier_semaphore()
    greeted = [dev_s, dev_xhi, dev_zp, dev_zm] + dev_peers
    greeted += [((gx + d) % 8, gy, zo) for d in (1, 2, 6, 7)]
    for other in greeted:
        pl.semaphore_signal(barrier, inc=1, device_id=other, device_id_type=MESH)
    pl.semaphore_wait(barrier, len(greeted))

    sent = []

    def send(name, c, src, dst, to):
        copy = pltpu.make_async_remote_copy(
            src_ref=src, dst_ref=dst, send_sem=send_sem.at[TYPES[name], c], recv_sem=recv_sem.at[TYPES[name], c],
            device_id=to, device_id_type=MESH,
        )
        copy.start()
        sent.append(copy)

    def came(name, c, dst):
        pltpu.make_async_remote_copy(
            src_ref=dst, dst_ref=dst, send_sem=send_sem.at[TYPES[name], c], recv_sem=recv_sem.at[TYPES[name], c],
            device_id=dev_s, device_id_type=MESH,
        ).wait_recv()

    def step_a0(c):
        copies["hid%d" % c].wait()
        own = g.at[c, xhi, core, z]
        send("a_x", c, own, own, dev_xhi)
        send("a_zp", c, own, own, dev_zp)
        send("a_zm", c, own, own, dev_zm)
        send("a_s", c, own, own, dev_s)

    def step_a1(c):
        block = g.at[c, oxhi, core, z]
        came("a_x", c, block)
        send("a_xzp", c, block, block, dev_zp)
        send("a_xzm", c, block, block, dev_zm)
        send("a_xs", c, block, block, dev_s)

    def step_a2(c):
        came("a_zp", c, g.at[c, xhi, core, zm])
        came("a_xzp", c, g.at[c, oxhi, core, zm])
        relay = g.at[c, 0, core, zm]
        send("a_rp", c, relay, relay, dev_zp)
        came("a_zm", c, g.at[c, xhi, core, zp])
        came("a_xzm", c, g.at[c, oxhi, core, zp])
        relay = g.at[c, 1, core, zp]
        send("a_rm", c, relay, relay, dev_zm)
        both = g.at[c, :, core, zm]
        send("a_sm", c, both, both, dev_s)
        both = g.at[c, :, core, zp]
        send("a_sp", c, both, both, dev_s)

    def step_a3(c):
        came("a_rp", c, g.at[c, 0, core, z2])
        came("a_rm", c, g.at[c, 1, core, z2])
        both = g.at[c, :, core, z2]
        send("a_s2", c, both, both, dev_s)

    def step_dq(_):
        rows = lax.broadcasted_iota(jnp.int32, (16, QC), 0)
        cols = lax.broadcasted_iota(jnp.int32, (16, QC), 1)
        spread = jnp.where(rows == cols // 64, 1.0, 0.0).astype(BF16)
        powers = jnp.exp2(qe[...].astype(F32)).astype(BF16)
        scale_q[...] = jnp.dot(powers, spread, preferred_element_type=F32) * (1.0 / 128.0)
        copies["kc"].wait()
        lane = lax.broadcasted_iota(jnp.int32, (1, 128), 1)

        def key_block(k, carry):
            at = pl.multiple_of(k * 128, 128)
            e = jnp.where(lane < 64, ke[0, k], ke[1, k]).astype(F32)
            scale = jnp.exp2(e) * (1.0 / 128.0)
            block = kct[:, pl.ds(at, 128)].astype(F32).T
            wk[pl.ds(at, 128), :] = (block * scale).astype(BF16)
            return carry

        lax.fori_loop(0, 16, key_block, 0)
        copies["qc"].wait()

        def query_block(k, carry):
            at = pl.multiple_of(k * 128, 128)
            scale = scale_q[pl.ds(k, 1), :]
            wq[pl.ds(at, 128), :] = (wq[pl.ds(at, 128), :].astype(F32) * scale).astype(BF16)
            return carry

        lax.fori_loop(0, 16, query_block, 0)
        sums[...] = jnp.zeros_like(sums)

    def step_do(_):
        rows = lax.broadcasted_iota(jnp.int32, (32, FEAT), 0)
        cols = lax.broadcasted_iota(jnp.int32, (32, FEAT), 1)
        spread = jnp.where(rows == cols // 64, 1.0, 0.0).astype(BF16)
        powers = jnp.exp2(oe[...].astype(F32)).astype(BF16)
        scale_o[...] = jnp.dot(powers, spread, preferred_element_type=F32) * (1.0 / 128.0)
        copies["oc"].wait()

        def output_block(k, carry):
            at = pl.multiple_of(k * 128, 128)
            scale = scale_o[pl.ds(k, 1), :]
            wo[pl.ds(at, 128), :] = (wo[pl.ds(at, 128), :].astype(F32) * scale).astype(BF16)
            return carry

        lax.fori_loop(0, 8, output_block, 0)

    def step_mm(c):
        came("a_s", c, g.at[c, xhi, ocore, z])
        came("a_xs", c, g.at[c, oxhi, ocore, z])
        came("a_sm", c, g.at[c, :, ocore, zm])
        came("a_sp", c, g.at[c, :, ocore, zp])
        came("a_s2", c, g.at[c, :, ocore, z2])
        weight = gain[...].astype(F32)

        def scaled(p, carry):
            block = g[c, p // 8, (p // 4) % 2, p % 4].astype(F32)
            at = pl.multiple_of(p * 16, 16)
            x[pl.ds(at, 16), :] = (block * weight).astype(BF16)
            total = block[:, :128] * block[:, :128]
            for k in range(1, FEAT // 128):
                piece = block[:, k * 128:(k + 1) * 128]
                total = total + piece * piece
            squares[pl.ds(at, 16), :] = total
            return carry

        lax.fori_loop(0, 16, scaled, 0)
        sums[c:c + 1, :] = jnp.sum(squares[...].T, axis=0, keepdims=True)

        def columns(n, carry):
            at = pl.multiple_of(n * 256, 256)
            part = jnp.dot(x[...], wq[:, pl.ds(at, 256)], preferred_element_type=F32)
            qp[c, :, :, :, pl.ds(at, 256)] = part.astype(BF16).reshape(2, 4, 32, 256)
            return carry

        lax.fori_loop(0, QC // 256, columns, 0)
        part = jnp.dot(x[...], wk[...], preferred_element_type=F32)
        qp[c, :, :, :, QC:] = part.astype(BF16).reshape(2, 4, 32, 128)
        send("b_2p", c, qp.at[c, 0, y2], b2.at[c, 0], dev_yp)
        send("b_2m", c, qp.at[c, 1, y2], b2.at[c, 1], dev_ym)
        send("b_1p", c, qp.at[c, 1, yp], b3.at[c, 1, 0], dev_yp)
        send("b_1m", c, qp.at[c, 0, ym], b3.at[c, 0, 1], dev_ym)

    def step_b2(c):
        came("b_2p", c, b2.at[c, 0])
        bu[c, 0] = qp[c, 0, yp] + b2[c, 0]
        send("b_sp", c, bu.at[c, 0], b3.at[c, 0, 0], dev_yp)
        came("b_2m", c, b2.at[c, 1])
        bu[c, 1] = qp[c, 1, ym] + b2[c, 1]
        send("b_sm", c, bu.at[c, 1], b3.at[c, 1, 1], dev_ym)

    def step_b3(c):
        came("b_1p", c, b3.at[c, 1, 0])
        came("b_1m", c, b3.at[c, 0, 1])
        came("b_sp", c, b3.at[c, 0, 0])
        came("b_sm", c, b3.at[c, 1, 1])
        total = qp[c, oxlo, y].astype(F32) + b3[c, oxlo, 0].astype(F32) + b3[c, oxlo, 1].astype(F32)
        bx[c] = total.astype(BF16)
        send("b_x", c, bx.at[c], b4.at[c], dev_xlo)
        qown[c] = qp[c, xlo, y].astype(F32) + b3[c, xlo, 0].astype(F32) + b3[c, xlo, 1].astype(F32)

    def step_b4(c):
        came("b_x", c, b4.at[c])
        qown[c] = qown[c] + b4[c].astype(F32)

    def step_ss(_):
        for i, to in enumerate(dev_peers):
            copy = pltpu.make_async_remote_copy(
                src_ref=sums, dst_ref=sums_in.at[i], send_sem=s_send.at[i], recv_sem=s_recv.at[i],
                device_id=to, device_id_type=MESH,
            )
            copy.start()
            sent.append(copy)

    def rotated(field, d):
        return field * cos[d] + pltpu.roll(field, 64, 1) * sin[d]

    def attention():
        total = sums[...]
        for i in range(len(peers)):
            pltpu.make_async_remote_copy(
                src_ref=sums, dst_ref=sums_in.at[i], send_sem=s_send.at[i], recv_sem=s_recv.at[i],
                device_id=dev_s, device_id_type=MESH,
            ).wait_recv()
            total = total + sums_in[i]
        inverse = lax.rsqrt(total * (1.0 / D) + EPS)
        lane = lax.broadcasted_iota(jnp.int32, (32, 256), 1)
        row = lax.broadcasted_iota(jnp.int32, (32, 256), 0)
        factors = []
        for c in range(NC):
            spread = jnp.where(lane == row + 32 * gx, inverse[c:c + 1, :], 0.0)
            factors.append(jnp.sum(spread, axis=1, keepdims=True))
        for c in range(NC):
            own = (qown[c, :, QC:] * factors[c]).astype(BF16)
            kv[0, 0, :, c] = own.reshape(2, 16, 128)
        for i, (d, other, to) in enumerate(dev_kv):
            copy = pltpu.make_async_remote_copy(
                src_ref=kv.at[0, 0], dst_ref=kv.at[d, other], send_sem=k_send.at[i], recv_sem=k_recv.at[i],
                device_id=to, device_id_type=MESH,
            )
            copy.start()
            sent.append(copy)
        for d in range(3):
            copies["cos%d" % d].wait()
            copies["sin%d" % d].wait()
        scaled = [qown[c, :, :QC] * factors[c] for c in range(NC)]
        for h in range(8):
            parts = [scaled[c][:, h * 128:(h + 1) * 128].reshape(2, 1, 16, 128) for c in range(NC)]
            head = jnp.concatenate(parts, axis=1).reshape(128, 128)
            qr[h] = rotated(head, 0).astype(BF16)
        for i, (d, other, to) in enumerate(dev_kv):
            pltpu.make_async_remote_copy(
                src_ref=kv.at[0, 0], dst_ref=kv.at[d, other], send_sem=k_send.at[i], recv_sem=k_recv.at[i],
                device_id=dev_s, device_id_type=MESH,
            ).wait_recv()
        low = lax.broadcasted_iota(jnp.int32, (128, 128), 1) < 64
        for d in range(3):
            at = (2 - d) * 128
            first = kv[d, odd].reshape(128, 128).astype(F32)
            second = kv[d, 1 - odd].reshape(128, 128).astype(F32)
            keys = jnp.where(low, first, pltpu.roll(second, 64, 1))
            kb[at:at + 128, :] = rotated(keys, d).astype(BF16)
            vb[at:at + 128, :] = jnp.where(low, pltpu.roll(first, 64, 1), second).astype(BF16)
        key_segments = jnp.concatenate([segs[pl.ds((gx + 8 - d) % 8, 1), :] for d in (2, 1, 0)], axis=1)
        lane = lax.broadcasted_iota(jnp.int32, (128, 128), 1)
        row = lax.broadcasted_iota(jnp.int32, (128, 128), 0)
        mine = segs[pl.ds(gx, 1), :].astype(F32)
        query_segments = jnp.sum(jnp.where(lane == row, mine, 0.0), axis=1, keepdims=True)
        place = lax.broadcasted_iota(jnp.int32, (128, 384), 1)
        row = lax.broadcasted_iota(jnp.int32, (128, 384), 0)
        allowed = (query_segments == key_segments.astype(F32)) & (place <= row + 256) & (place >= 256 - 128 * gx)
        for h in range(8):
            scores = lax.dot_general(qr[h], kb[...], (((1,), (1,)), ((), ())), preferred_element_type=F32)
            scores = jnp.where(allowed, scores * (1.0 / math.sqrt(HD)), -jnp.inf)
            weights = jnp.exp(scores - jnp.max(scores, axis=1, keepdims=True))
            weights = (weights / jnp.sum(weights, axis=1, keepdims=True)).astype(BF16)
            head = jnp.dot(weights, vb[...], preferred_element_type=F32).astype(BF16).reshape(2, 4, 16, 128)
            for c in range(NC):
                ag[c, xlo, y, :, :, h * 128:(h + 1) * 128] = head[:, c]

    def step_c0(c):
        own = ag.at[c, xlo, y]
        send("c_x", c, own, own, dev_xlo)
        send("c_yp", c, own, own, dev_yp)
        send("c_ym", c, own, own, dev_ym)

    def step_c1(c):
        block = ag.at[c, oxlo, y]
        came("c_x", c, block)
        send("c_xyp", c, block, block, dev_yp)
        send("c_xym", c, block, block, dev_ym)

    def step_c2(c):
        came("c_yp", c, ag.at[c, xlo, ym])
        came("c_xyp", c, ag.at[c, oxlo, ym])
        relay = ag.at[c, 0, ym]
        send("c_rp", c, relay, relay, dev_yp)
        came("c_ym", c, ag.at[c, xlo, yp])
        came("c_xym", c, ag.at[c, oxlo, yp])
        relay = ag.at[c, 1, yp]
        send("c_rm", c, relay, relay, dev_ym)

    def step_c3(c):
        came("c_rp", c, ag.at[c, 0, y2])
        came("c_rm", c, ag.at[c, 1, y2])

    def step_mo(c):
        rows = ag[c].reshape(256, QC)

        def columns(n, carry):
            at = pl.multiple_of(n * 256, 256)
            part = jnp.dot(rows, wo[:, pl.ds(at, 256)], preferred_element_type=F32)
            pp[c, :, :, :, :, pl.ds(at, 256)] = part.astype(BF16).reshape(2, 2, 4, 16, 256)
            return carry

        lax.fori_loop(0, FEAT // 256, columns, 0)
        send("d_s", c, pp.at[c, :, ocore], d_in.at[c], dev_s)

    def step_d1(c):
        came("d_s", c, d_in.at[c])

        def add(w):
            for h in range(2):
                dt[c, h, w] = pp[c, h, core, w] + d_in[c, h, w]

        add(z2)
        send("d_2p", c, dt.at[c, 0, z2], d2.at[c, 0], dev_zp)
        send("d_2m", c, dt.at[c, 1, z2], d2.at[c, 1], dev_zm)
        add(zp)
        send("d_1p", c, dt.at[c, 1, zp], d3.at[c, 1, 0], dev_zp)
        add(zm)
        send("d_1m", c, dt.at[c, 0, zm], d3.at[c, 0, 1], dev_zm)
        add(z)

    def step_d2(c):
        came("d_2p", c, d2.at[c, 0])
        du[c, 0] = dt[c, 0, zp] + d2[c, 0]
        send("d_sp", c, du.at[c, 0], d3.at[c, 0, 0], dev_zp)
        came("d_2m", c, d2.at[c, 1])
        du[c, 1] = dt[c, 1, zm] + d2[c, 1]
        send("d_sm", c, du.at[c, 1], d3.at[c, 1, 1], dev_zm)

    def step_d3(c):
        came("d_1p", c, d3.at[c, 1, 0])
        came("d_1m", c, d3.at[c, 0, 1])
        came("d_sp", c, d3.at[c, 0, 0])
        came("d_sm", c, d3.at[c, 1, 1])
        total = dt[c, oxhi, z].astype(F32) + d3[c, oxhi, 0].astype(F32) + d3[c, oxhi, 1].astype(F32)
        dx[c] = total.astype(BF16)
        send("d_x", c, dx.at[c], d4.at[c], dev_xhi)
        total = dt[c, xhi, z].astype(F32) + d3[c, xhi, 0].astype(F32) + d3[c, xhi, 1].astype(F32)
        down[c] = total + g[c, xhi, core, z].astype(F32)

    def step_d4(c):
        came("d_x", c, d4.at[c])
        out[16 * c:16 * c + 16, :] = (down[c] + d4[c].astype(F32)).astype(BF16)

    table = {
        "A0": step_a0, "A1": step_a1, "A2": step_a2, "A3": step_a3, "DQ": step_dq, "DO": step_do, "MM": step_mm,
        "B2": step_b2, "B3": step_b3, "B4": step_b4, "SS": step_ss, "C0": step_c0, "C1": step_c1, "C2": step_c2,
        "C3": step_c3, "MO": step_mo, "D1": step_d1, "D2": step_d2, "D3": step_d3, "D4": step_d4,
    }
    for name, c in FIRST:
        table[name](c)
    attention()
    for name, c in SECOND:
        table[name](c)
    for copy in sent:
        copy.wait_send()


def shards(hid, gain, segs, qc, qe, kc, ke, oc, oe):
    cosine, sine = rope_tables()
    kct = kc.transpose(1, 2, 0).reshape(128, FEAT)
    ket = ke.transpose(1, 2, 0).reshape(2, 16)
    hbm, vmem, smem = (pl.BlockSpec(memory_space=m) for m in (pl.ANY, pltpu.VMEM, pltpu.SMEM))
    types = len(TYPES)
    scratch = [
        ((FEAT, QC), BF16), ((FEAT, 128), BF16), ((QC, FEAT), BF16), ((128, FEAT), BF16),
        ((16, QC), F32), ((8, FEAT), F32), ((3, 128, HD), F32), ((3, 128, HD), F32),
        ((NC, 2, 2, 4, 16, FEAT), BF16), ((256, FEAT), BF16), ((256, 128), F32), ((8, 256), F32), ((7, 8, 256), F32),
        ((NC, 2, 4, 32, QW), BF16), ((NC, 2, 32, QW), BF16), ((NC, 2, 32, QW), BF16),
        ((NC, 2, 2, 32, QW), BF16), ((NC, 32, QW), BF16), ((NC, 32, QW), BF16), ((NC, 32, QW), F32),
        ((3, 2, 2, 4, 16, 128), BF16), ((384, 128), BF16), ((384, 128), BF16), ((8, 128, 128), BF16),
        ((NC, 2, 4, 2, 16, QC), BF16), ((NC, 2, 2, 4, 16, FEAT), BF16), ((NC, 2, 4, 16, FEAT), BF16),
        ((NC, 2, 4, 16, FEAT), BF16), ((NC, 2, 16, FEAT), BF16), ((NC, 2, 16, FEAT), BF16),
        ((NC, 2, 2, 16, FEAT), BF16), ((NC, 16, FEAT), BF16), ((NC, 16, FEAT), BF16), ((NC, 16, FEAT), F32),
    ]
    scratch = [pltpu.VMEM(shape, dtype) for shape, dtype in scratch]
    dma = pltpu.SemaphoreType.DMA
    scratch += [dma((types, NC)), dma((types, NC)), dma((7,)), dma((7,)), dma((5,)), dma((5,)), dma((13,))]
    return pl.pallas_call(
        layer,
        out_shape=jax.ShapeDtypeStruct((64, FEAT), BF16),
        in_specs=[hbm, vmem, vmem, hbm, vmem, hbm, smem, hbm, vmem, hbm, hbm],
        out_specs=vmem,
        scratch_shapes=scratch,
        compiler_params=pltpu.CompilerParams(collective_id=0, has_side_effects=True, vmem_limit_bytes=60 * 1024 * 1024),
        name="layer",
    )(hid, gain.reshape(1, FEAT), segs.reshape(8, 128), qc, qe, kct, ket, oc, oe, jnp.asarray(cosine), jnp.asarray(sine))


def solution(mesh):
    placed = (
        P(("gy", "gz"), "gx"),
        P("gx"),
        P(),
        P("gx", ("gy", "gz")),
        P("gx", ("gy", "gz")),
        P("gx", None, ("gy", "gz")),
        P("gx", None, ("gy", "gz")),
        P(("gy", "gz"), "gx"),
        P(("gy", "gz"), "gx"),
    )
    return jax.shard_map(shards, mesh=mesh, in_specs=placed, out_specs=P(("gy", "gz"), "gx"), check_vma=False)
```

time: 359 us -> 120 us (0.33)
  waiting for transfers between devices: 264 us -> 0 us
  Pallas kernels: 0 us -> 116 us
  matrix products: 26.2 us -> 0 us
  other arithmetic: 17.1 us -> 0 us
  blocking collectives: 17 us -> 0 us
  local copies, waits for them, and re-layouts: 18.7 us -> 2.96 us
  between operations: 13.3 us -> 0.01 us
    reduce_scatter x2 -> x0, waiting for transfers between devices: 122 us -> none  [the longest x1 85 us: shards(): lax.psum_scatter(jnp.dot(gathered, output_weight, preferred_element_type=...]
    pallas_call x0 -> x1, Pallas kernels: none -> 116 us  [shards(): pl.pallas_call(layer, out_shape=jax.ShapeDtypeStruct((64, FEAT), BF16), i...]
    all_gather x2 -> x0, waiting for transfers between devices: 81.1 us -> none  [the longest x1 42.7 us: shards(): everyone = lax.all_gather(normed, ('gy', 'gz'), axis=0, tiled=True)]
    psum x1 -> x0, waiting for transfers between devices: 56.9 us -> none  [shards(): key_value = lax.psum(key_part.astype(jnp.bfloat16), 'gx')]
    dot_general x4 -> x0, matrix products: 22.8 us -> none  [the longest x1 8.56 us: shards(): jnp.dot(everyone, query_weight, preferred_element_type=jnp.float32)]
    psum x1 -> x0, blocking collectives: 17 us -> none  [shards(): squares = lax.psum(partial_squares, 'gx')]
    unnamed x18 -> x1, local copies, waits for them, and re-layouts: 16.9 us -> 1.67 us
    convert_element_type x7 -> x0, other arithmetic: 11.5 us -> none  [the longest x1 6.22 us: dequant_matrix(): (scaled.reshape(rows_all, cols_all) * (1.0 / math.sqrt(fan_in))).astype(j...]
  transfers between devices with their start and end apart: 6 -> 0, of which waited for: 6 -> 0; matrix products, arithmetic and copies ran while one was open for 9% -> 0% of each run, Pallas kernels for 0% -> 0%
where the time goes in v1:
time: 120 us; the launch traced here: 119 us
  Pallas kernels  116 us (97%)
  local copies, waits for them, and re-layouts  2.96 us (2%)
    pallas_call x1, Pallas kernels, shards(): pl.pallas_call(layer, out_shape=jax.ShapeDtypeStruct((64, FEAT), BF16), i...  116 us

profile of v1, /device:TPU:1, one launch (start us, length us, event | category | flops | bytes accessed | tf_op | source)
XLA Modules:
  0.0 119.2 jit_solution(12813282772573522805)
XLA Ops:
  0.0 1.3 %reshape.12.gain = bf16[1,2048]{1,0:T(2,128)(2,1)} reshape(bf16[2048]{0:T(1024)(128)(2,1)} %param.12) | data formatting | bytes 8192 | tf_op jit(solution)/shard_map/reshape | solution.py:449
  1.3 116.2 %layer.1 = bf16[64,2048]{1,0:T(8,128)(2,1)} custom-call(bf16[64,2048]{1,0:T(8,128)(2,1)} %hid.1, bf16[1,2048]{1,0:T(2,128)(2,1)} %reshape.12.gain, s32[8,128]{1,0:T(8,128)} %bitcast.8, bf16[2048,1024]{1,0:T(8,128)(2,1)} %qc.1, s32[16,16]{1,0:T(8,128)} %qe.1, bf16[128,2048]{1,0:T(8,128)(2,1)} %bitcast.7, s32[2,16]{1,0:T(2,128)} %bitcast.9, ...), custom_call_target="tpu_custom_call" | custom-call | tf_op jit(solution)/shard_map/layer/pallas_call | solution.py:441
  117.5 1.7 %copy.13 = bf16[64,2048]{1,0:T(8,128)(2,1)} copy(bf16[64,2048]{1,0:T(8,128)(2,1)} %layer.1) | data formatting | bytes 524288

commit v2 on v1

v2 whole, which is shorter than its diff:
```python
import math

import jax
import jax.numpy as jnp
import numpy as np
from jax import lax
from jax.experimental import pallas as pl
from jax.experimental.pallas import tpu as pltpu
from jax.sharding import PartitionSpec as P

D = 16384
HD = 128
TOKENS = 1024
THETA = 500000.0
EPS = 1e-05
NC = 4
FEAT = 2048
QC = 1024
QH, OH = 512, 1024
F32, BF16 = jnp.float32, jnp.bfloat16
MESH = pl.DeviceIdType.MESH

UNITS = 2
TYPES = ["a_x", "a_zp", "a_zm", "a_s", "a_xzp", "a_xzm", "a_xs", "a_rp", "a_rm", "a_sm", "a_sp", "a_s2"]
TYPES += ["b_2p", "b_2m", "b_x", "b_p", "b_p_cross", "b_m", "b_m_cross"]
TYPES += ["c_x", "c_yp", "c_ym", "c_xyp", "c_xym", "c_rp", "c_rm"]
TYPES += ["d_s", "d_2p", "d_2m", "d_x", "d_p", "d_p_cross", "d_m", "d_m_cross"]
TYPES = {name: i for i, name in enumerate(TYPES)}

ORDER = (
    ("A0", 0), ("A0", 1), ("A1", 0), ("A0", 2), ("A1", 1), ("A2", 0), ("A1", 2), ("DQ", 0), ("A2", 1), ("A0", 3),
    ("A3", 0), ("HG", 0), ("A1", 3), ("MM", 0), ("A3", 1), ("A2", 2), ("MM", 1), ("HG", 1), ("A2", 3), ("B2", 0),
    ("MM", 11), ("A3", 2), ("MM", 10), ("B2", 1), ("HG", 2), ("A3", 3), ("B2", 11), ("MM", 20), ("HG", 3),
    ("KS", 0), ("DO", 0), ("B2", 10), ("MM", 21), ("B4", 0), ("B2", 20), ("KX", 0), ("MM", 31), ("MM", 30),
    ("B4", 10), ("B4", 1), ("B2", 21), ("KY", 0), ("B2", 31), ("AT", 0), ("B4", 11), ("AT", 1), ("B2", 30),
    ("B4", 20), ("C1", 0), ("B4", 21), ("C1", 1), ("AT", 2), ("C2", 0), ("C2", 1), ("B4", 31), ("B4", 30),
    ("C1", 2), ("AT", 3), ("C3", 0), ("MO", 1), ("C3", 1), ("MO", 11), ("D1", 1), ("C2", 2), ("MO", 10), ("C1", 3),
    ("D1", 11), ("MO", 0), ("D2", 1), ("D1", 10), ("C3", 2), ("MO", 20), ("D2", 11), ("C2", 3), ("D1", 0),
    ("MO", 21), ("D4", 1), ("D1", 20), ("D1", 21), ("D2", 10), ("C3", 3), ("D2", 0), ("MO", 31), ("MO", 30),
    ("D1", 31), ("D1", 30), ("D2", 20), ("D2", 21), ("D2", 31), ("D2", 30), ("D4", 0), ("D4", 21), ("D4", 10),
    ("D4", 20), ("D4", 11), ("D4", 31), ("D4", 30),
)


def rope_tables():
    frequency = np.exp(np.arange(HD // 2, dtype=np.float64) * (-2.0 * math.log(THETA) / HD))
    angles = np.arange(TOKENS, dtype=np.float64)[:, None] * frequency[None, :]
    cosine, sine = np.cos(angles), np.sin(angles)
    cosine = np.concatenate([cosine, cosine], axis=1).astype(np.float32)
    sine = np.concatenate([-sine, sine], axis=1).astype(np.float32)
    return cosine.reshape(8, 128, HD), sine.reshape(8, 128, HD)


def layer(
    hid, gain, segs, qc, qe, kc, ke, oc, oe, cos_hbm, sin_hbm, out,
    wq, wk, wo, kct, scale_q, scale_o, cos, sin,
    g, x, squares, sums, sums_in, factors,
    qp, b2, bu, b3, bx, qown,
    kvp, kv_in, kv, kb, vb, qr,
    ag, pp, d_in, dt, d2, du, d3, dx,
    send_sem, recv_sem, s_send, s_recv, p_send, p_recv, k_send, k_recv, local,
):
    gx, gy, gz = lax.axis_index("gx"), lax.axis_index("gy"), lax.axis_index("gz")
    xlo, y, xhi, core, z = gx // 4, gx % 4, gy // 2, gy % 2, gz
    yp, ym, y2 = (y + 1) % 4, (y + 3) % 4, (y + 2) % 4
    zp, zm, z2 = (z + 1) % 4, (z + 3) % 4, (z + 2) % 4
    oxlo, oxhi, ocore = 1 - xlo, 1 - xhi, 1 - core
    odd = z % 2
    zo = z + 1 - 2 * odd
    dev_s = (gx, xhi * 2 + ocore, gz)
    dev_xhi = (gx, oxhi * 2 + core, gz)
    dev_zp, dev_zm = (gx, gy, zp), (gx, gy, zm)
    dev_xlo = (oxlo * 4 + y, gy, gz)
    dev_yp, dev_ym = (xlo * 4 + yp, gy, gz), (xlo * 4 + ym, gy, gz)
    peers = [(a, b) for a in range(2) for b in range(4) if (a, b) != (0, 0)]
    dev_peers = [(((xlo + a) % 2) * 4 + (y + b) % 4, gy, gz) for a, b in peers]
    dev_kv = [(0, 1, (gx, gy, zo))]
    for d in (1, 2):
        dev_kv += [(d, 0, ((gx + d) % 8, gy, z)), (d, 1, ((gx + d) % 8, gy, zo))]

    copies = {}

    def fetch(name, index, src, dst):
        copies[name] = pltpu.make_async_copy(src, dst, local.at[index])
        copies[name].start()

    for c in range(NC):
        fetch("hid%d" % c, c, hid.at[pl.ds(16 * c, 16), :], g.at[c, xhi, core, z])
    fetch("kc", 4, kc, kct)
    fetch("qc", 5, qc, wq)
    for d in range(3):
        fetch("cos%d" % d, 6 + d, cos_hbm.at[(gx + 8 - d) % 8], cos.at[d])
        fetch("sin%d" % d, 9 + d, sin_hbm.at[(gx + 8 - d) % 8], sin.at[d])
    fetch("oc", 12, oc, wo)

    barrier = pltpu.get_barrier_semaphore()
    greeted = [dev_s, dev_xhi, dev_zp, dev_zm, (gx, oxhi * 2 + core, zp), (gx, oxhi * 2 + core, zm)] + dev_peers
    greeted += [((gx + d) % 8, gy, zo) for d in (1, 2, 6, 7)]
    for other in greeted:
        pl.semaphore_signal(barrier, inc=1, device_id=other, device_id_type=MESH)
    pl.semaphore_wait(barrier, len(greeted))

    sent = []

    def send(name, c, src, dst, to, cross=0):
        copy = pltpu.make_async_remote_copy(
            src_ref=src, dst_ref=dst, send_sem=send_sem.at[TYPES[name] + cross, c],
            recv_sem=recv_sem.at[TYPES[name] + cross, c], device_id=to, device_id_type=MESH,
        )
        copy.start()
        sent.append(copy)

    def came(name, c, dst):
        pltpu.make_async_remote_copy(
            src_ref=dst, dst_ref=dst, send_sem=send_sem.at[TYPES[name], c], recv_sem=recv_sem.at[TYPES[name], c],
            device_id=dev_s, device_id_type=MESH,
        ).wait_recv()

    def send_some(src, dst, sends, recvs, i, to):
        copy = pltpu.make_async_remote_copy(
            src_ref=src, dst_ref=dst, send_sem=sends.at[i], recv_sem=recvs.at[i], device_id=to, device_id_type=MESH,
        )
        copy.start()
        sent.append(copy)

    def came_some(dst, sends, recvs, i):
        pltpu.make_async_remote_copy(
            src_ref=dst, dst_ref=dst, send_sem=sends.at[i], recv_sem=recvs.at[i], device_id=dev_s, device_id_type=MESH,
        ).wait_recv()

    def step_a0(c):
        copies["hid%d" % c].wait()
        own = g.at[c, xhi, core, z]
        send("a_x", c, own, own, dev_xhi)
        send("a_zp", c, own, own, dev_zp)
        send("a_zm", c, own, own, dev_zm)
        send("a_s", c, own, own, dev_s)

    def step_a1(c):
        block = g.at[c, oxhi, core, z]
        came("a_x", c, block)
        send("a_xzp", c, block, block, dev_zp)
        send("a_xzm", c, block, block, dev_zm)
        send("a_xs", c, block, block, dev_s)

    def step_a2(c):
        came("a_zp", c, g.at[c, xhi, core, zm])
        came("a_xzp", c, g.at[c, oxhi, core, zm])
        relay = g.at[c, 0, core, zm]
        send("a_rp", c, relay, relay, dev_zp)
        came("a_zm", c, g.at[c, xhi, core, zp])
        came("a_xzm", c, g.at[c, oxhi, core, zp])
        relay = g.at[c, 1, core, zp]
        send("a_rm", c, relay, relay, dev_zm)
        both = g.at[c, :, core, zm]
        send("a_sm", c, both, both, dev_s)
        both = g.at[c, :, core, zp]
        send("a_sp", c, both, both, dev_s)

    def step_a3(c):
        came("a_rp", c, g.at[c, 0, core, z2])
        came("a_rm", c, g.at[c, 1, core, z2])
        both = g.at[c, :, core, z2]
        send("a_s2", c, both, both, dev_s)

    def step_dq(_):
        rows = lax.broadcasted_iota(jnp.int32, (16, QC), 0)
        cols = lax.broadcasted_iota(jnp.int32, (16, QC), 1)
        spread = jnp.where(rows == cols // 64, 1.0, 0.0).astype(BF16)
        powers = jnp.exp2(qe[...].astype(F32)).astype(BF16)
        scale_q[...] = jnp.dot(powers, spread, preferred_element_type=F32) * (1.0 / 128.0)
        copies["kc"].wait()
        lane = lax.broadcasted_iota(jnp.int32, (1, 128), 1)

        def key_block(k, carry):
            at = pl.multiple_of(k * 128, 128)
            e = jnp.where(lane < 64, ke[0, k], ke[1, k]).astype(F32)
            scale = jnp.exp2(e) * (1.0 / 128.0)
            block = kct[:, pl.ds(at, 128)].astype(F32).T
            wk[pl.ds(at, 128), :] = (block * scale).astype(BF16)
            return carry

        lax.fori_loop(0, 16, key_block, 0)
        copies["qc"].wait()

        def query_block(k, carry):
            at = pl.multiple_of(k * 128, 128)
            scale = scale_q[pl.ds(k, 1), :]
            wq[pl.ds(at, 128), :] = (wq[pl.ds(at, 128), :].astype(F32) * scale).astype(BF16)
            return carry

        lax.fori_loop(0, 16, query_block, 0)
        sums[...] = jnp.zeros_like(sums)

    def step_do(_):
        rows = lax.broadcasted_iota(jnp.int32, (32, FEAT), 0)
        cols = lax.broadcasted_iota(jnp.int32, (32, FEAT), 1)
        spread = jnp.where(rows == cols // 64, 1.0, 0.0).astype(BF16)
        powers = jnp.exp2(oe[...].astype(F32)).astype(BF16)
        scale_o[...] = jnp.dot(powers, spread, preferred_element_type=F32) * (1.0 / 128.0)
        copies["oc"].wait()

        def output_block(k, carry):
            at = pl.multiple_of(k * 128, 128)
            scale = scale_o[pl.ds(k, 1), :]
            wo[pl.ds(at, 128), :] = (wo[pl.ds(at, 128), :].astype(F32) * scale).astype(BF16)
            return carry

        lax.fori_loop(0, 8, output_block, 0)

    def step_hg(c):
        came("a_s", c, g.at[c, xhi, ocore, z])
        came("a_xs", c, g.at[c, oxhi, ocore, z])
        came("a_sm", c, g.at[c, :, ocore, zm])
        came("a_sp", c, g.at[c, :, ocore, zp])
        came("a_s2", c, g.at[c, :, ocore, z2])
        weight = gain[...].astype(F32)

        def scaled(p, carry):
            block = g[c, p // 8, (p // 4) % 2, p % 4].astype(F32)
            at = pl.multiple_of(p * 16, 16)
            x[c, pl.ds(at, 16), :] = (block * weight).astype(BF16)
            total = block[:, :128] * block[:, :128]
            for k in range(1, FEAT // 128):
                piece = block[:, k * 128:(k + 1) * 128]
                total = total + piece * piece
            squares[pl.ds(at, 16), :] = total
            return carry

        lax.fori_loop(0, 16, scaled, 0)
        sums[c:c + 1, :] = jnp.sum(squares[...].T, axis=0, keepdims=True)
        part = jnp.dot(x[c], wk[...], preferred_element_type=F32)
        kvp[:, :, :, c] = part.astype(BF16).reshape(2, 4, 2, 16, 128)

    def step_mm(k):
        c, u = k // 10, k % 10
        i = c * UNITS + u

        def columns(n, carry):
            at = pl.multiple_of(n * 256, 256)
            part = jnp.dot(x[c], wq[:, pl.ds(u * QH + at, 256)], preferred_element_type=F32)
            qp[c, u, :, :, :, pl.ds(at, 256)] = part.astype(BF16).reshape(2, 4, 32, 256)
            return carry

        lax.fori_loop(0, QH // 256, columns, 0)
        send("b_2p", i, qp.at[c, u, 0, y2], b2.at[c, u, 0], dev_yp)
        send("b_2m", i, qp.at[c, u, 1, y2], b2.at[c, u, 1], dev_ym)
        cross = (xlo + 1) % 2
        send("b_p", i, qp.at[c, u, 1, yp], b3.at[c, u, 0, cross], (4 + yp, gy, gz), cross)
        send("b_m", i, qp.at[c, u, 0, ym], b3.at[c, u, 1, xlo], (ym, gy, gz), xlo)
        send("b_x", i, qp.at[c, u, oxlo, y], bx.at[c, u], dev_xlo)

    def step_b2(k):
        c, u = k // 10, k % 10
        i = c * UNITS + u
        came("b_2p", i, b2.at[c, u, 0])
        bu[c, u, 0] = qp[c, u, 0, yp] + b2[c, u, 0]
        send("b_p", i, bu.at[c, u, 0], b3.at[c, u, 0, xlo], (yp, gy, gz), xlo)
        came("b_2m", i, b2.at[c, u, 1])
        bu[c, u, 1] = qp[c, u, 1, ym] + b2[c, u, 1]
        cross = (xlo + 1) % 2
        send("b_m", i, bu.at[c, u, 1], b3.at[c, u, 1, cross], (4 + ym, gy, gz), cross)

    def step_b4(k):
        c, u = k // 10, k % 10
        i = c * UNITS + u
        came("b_x", i, bx.at[c, u])
        came("b_p", i, b3.at[c, u, 0, 0])
        came("b_p_cross", i, b3.at[c, u, 0, 1])
        came("b_m", i, b3.at[c, u, 1, 0])
        came("b_m_cross", i, b3.at[c, u, 1, 1])
        total = qp[c, u, xlo, y].astype(F32) + bx[c, u].astype(F32)
        for direction in range(2):
            for column in range(2):
                total = total + b3[c, u, direction, column].astype(F32)
        qown[c, :, u * QH:(u + 1) * QH] = total

    def step_ks(_):
        for i, to in enumerate(dev_peers):
            send_some(sums, sums_in.at[i], s_send, s_recv, i, to)
            a, b = peers[i]
            send_some(kvp.at[(xlo + a) % 2, (y + b) % 4], kv_in.at[i], p_send, p_recv, i, to)

    def rows_of(table, c):
        return jnp.concatenate([table[c * 16:c * 16 + 16], table[64 + c * 16:64 + c * 16 + 16]], axis=0)

    def rotated(field, cosine, sine):
        return field * cosine + pltpu.roll(field, 64, 1) * sine

    def step_kx(_):
        total = sums[...]
        for i in range(len(peers)):
            came_some(sums_in.at[i], s_send, s_recv, i)
            total = total + sums_in[i]
        inverse = lax.rsqrt(total * (1.0 / D) + EPS)
        lane = lax.broadcasted_iota(jnp.int32, (32, 256), 1)
        row = lax.broadcasted_iota(jnp.int32, (32, 256), 0)
        for c in range(NC):
            spread = jnp.where(lane == row + 32 * gx, inverse[c:c + 1, :], 0.0)
            factors[c] = jnp.broadcast_to(jnp.sum(spread, axis=1, keepdims=True), (32, 128))
        for i in range(len(peers)):
            came_some(kv_in.at[i], p_send, p_recv, i)
        for c in range(NC):
            part = kvp[xlo, y, :, c].astype(F32)
            for i in range(len(peers)):
                part = part + kv_in[i, :, c].astype(F32)
            kv[0, 0, :, c] = (part.reshape(32, 128) * factors[c]).astype(BF16).reshape(2, 16, 128)
        for i, (d, other, to) in enumerate(dev_kv):
            send_some(kv.at[0, 0], kv.at[d, other], k_send, k_recv, i, to)

    def step_ky(_):
        for d in range(3):
            copies["cos%d" % d].wait()
            copies["sin%d" % d].wait()
        for i, (d, other, to) in enumerate(dev_kv):
            came_some(kv.at[d, other], k_send, k_recv, i)
        low = lax.broadcasted_iota(jnp.int32, (128, 128), 1) < 64
        for d in range(3):
            at = (2 - d) * 128
            first = kv[d, odd].reshape(128, 128).astype(F32)
            second = kv[d, 1 - odd].reshape(128, 128).astype(F32)
            keys = jnp.where(low, first, pltpu.roll(second, 64, 1))
            kb[at:at + 128, :] = rotated(keys, cos[d], sin[d]).astype(BF16)
            vb[at:at + 128, :] = jnp.where(low, pltpu.roll(first, 64, 1), second).astype(BF16)

    def step_at(c):
        cosine, sine = rows_of(cos[0], c), rows_of(sin[0], c)
        factor = factors[c]
        for h in range(8):
            head = qown[c, :, h * 128:(h + 1) * 128] * factor
            qr[h * 32:(h + 1) * 32, :] = rotated(head, cosine, sine).astype(BF16)
        row = lax.broadcasted_iota(jnp.int32, (32, 128), 0)
        lane = lax.broadcasted_iota(jnp.int32, (32, 128), 1)
        mine = segs[pl.ds(gx, 1), :].astype(F32)
        token = (row // 16) * 64 + c * 16 + row % 16
        query_segments = jnp.sum(jnp.where(lane == token, mine, 0.0), axis=1, keepdims=True)
        key_segments = jnp.concatenate([segs[pl.ds((gx + 8 - d) % 8, 1), :] for d in (2, 1, 0)], axis=1).astype(F32)
        row = lax.broadcasted_iota(jnp.int32, (32, 384), 0)
        place = lax.broadcasted_iota(jnp.int32, (32, 384), 1)
        token = (row // 16) * 64 + c * 16 + row % 16
        allowed = (query_segments == key_segments) & (place <= token + 256) & (place >= 256 - 128 * gx)
        masked = jnp.where(allowed, 0.0, -jnp.inf)
        scores = lax.dot_general(qr[...], kb[...], (((1,), (1,)), ((), ())), preferred_element_type=F32)
        scores = (scores * (1.0 / math.sqrt(HD))).reshape(8, 32, 384) + masked[None]
        weights = jnp.exp(scores - jnp.max(scores, axis=2, keepdims=True))
        weights = (weights / jnp.sum(weights, axis=2, keepdims=True)).astype(BF16).reshape(256, 384)
        heads = jnp.dot(weights, vb[...], preferred_element_type=F32).astype(BF16)
        for h in range(8):
            ag[c, xlo, y, :, :, h * 128:(h + 1) * 128] = heads[h * 32:(h + 1) * 32].reshape(2, 16, 128)
        own = ag.at[c, xlo, y]
        send("c_x", c, own, own, dev_xlo)
        send("c_yp", c, own, own, dev_yp)
        send("c_ym", c, own, own, dev_ym)

    def step_c1(c):
        block = ag.at[c, oxlo, y]
        came("c_x", c, block)
        send("c_xyp", c, block, block, dev_yp)
        send("c_xym", c, block, block, dev_ym)

    def step_c2(c):
        came("c_yp", c, ag.at[c, xlo, ym])
        came("c_xyp", c, ag.at[c, oxlo, ym])
        relay = ag.at[c, 0, ym]
        send("c_rp", c, relay, relay, dev_yp)
        came("c_ym", c, ag.at[c, xlo, yp])
        came("c_xym", c, ag.at[c, oxlo, yp])
        relay = ag.at[c, 1, yp]
        send("c_rm", c, relay, relay, dev_ym)

    def step_c3(c):
        came("c_rp", c, ag.at[c, 0, y2])
        came("c_rm", c, ag.at[c, 1, y2])

    def step_mo(k):
        c, u = k // 10, k % 10
        i = c * UNITS + u
        rows = ag[c].reshape(256, QC)

        def columns(n, carry):
            at = pl.multiple_of(n * 256, 256)
            part = jnp.dot(rows, wo[:, pl.ds(u * OH + at, 256)], preferred_element_type=F32)
            pp[c, u, :, :, :, :, pl.ds(at, 256)] = part.astype(BF16).reshape(2, 2, 4, 16, 256)
            return carry

        lax.fori_loop(0, OH // 256, columns, 0)
        send("d_s", i, pp.at[c, u, :, ocore], d_in.at[c, u], dev_s)

    def step_d1(k):
        c, u = k // 10, k % 10
        i = c * UNITS + u
        came("d_s", i, d_in.at[c, u])

        def add(w):
            for h in range(2):
                dt[c, u, h, w] = pp[c, u, h, core, w] + d_in[c, u, h, w]

        cross = (xhi + 1) % 2
        add(z2)
        send("d_2p", i, dt.at[c, u, 0, z2], d2.at[c, u, 0], dev_zp)
        send("d_2m", i, dt.at[c, u, 1, z2], d2.at[c, u, 1], dev_zm)
        add(zp)
        send("d_p", i, dt.at[c, u, 1, zp], d3.at[c, u, 0, cross], (gx, 2 + core, zp), cross)
        add(zm)
        send("d_m", i, dt.at[c, u, 0, zm], d3.at[c, u, 1, xhi], (gx, core, zm), xhi)
        add(z)
        send("d_x", i, dt.at[c, u, oxhi, z], dx.at[c, u], dev_xhi)

    def step_d2(k):
        c, u = k // 10, k % 10
        i = c * UNITS + u
        came("d_2p", i, d2.at[c, u, 0])
        du[c, u, 0] = dt[c, u, 0, zp] + d2[c, u, 0]
        send("d_p", i, du.at[c, u, 0], d3.at[c, u, 0, xhi], (gx, core, zp), xhi)
        came("d_2m", i, d2.at[c, u, 1])
        du[c, u, 1] = dt[c, u, 1, zm] + d2[c, u, 1]
        cross = (xhi + 1) % 2
        send("d_m", i, du.at[c, u, 1], d3.at[c, u, 1, cross], (gx, 2 + core, zm), cross)

    def step_d4(k):
        c, u = k // 10, k % 10
        i = c * UNITS + u
        came("d_x", i, dx.at[c, u])
        came("d_p", i, d3.at[c, u, 0, 0])
        came("d_p_cross", i, d3.at[c, u, 0, 1])
        came("d_m", i, d3.at[c, u, 1, 0])
        came("d_m_cross", i, d3.at[c, u, 1, 1])
        columns = slice(u * OH, (u + 1) * OH)
        total = dt[c, u, xhi, z].astype(F32) + dx[c, u].astype(F32)
        for direction in range(2):
            for column in range(2):
                total = total + d3[c, u, direction, column].astype(F32)
        own = g[c, xhi, core, z, :, columns].astype(F32)
        out[16 * c:16 * c + 16, columns] = (own + total).astype(BF16)

    table = {
        "A0": step_a0, "A1": step_a1, "A2": step_a2, "A3": step_a3, "DQ": step_dq, "DO": step_do, "HG": step_hg,
        "MM": step_mm, "B2": step_b2, "B4": step_b4, "KS": step_ks, "KX": step_kx, "KY": step_ky, "AT": step_at,
        "C1": step_c1, "C2": step_c2, "C3": step_c3, "MO": step_mo, "D1": step_d1, "D2": step_d2, "D4": step_d4,
    }
    for name, c in ORDER:
        table[name](c)
    for copy in sent:
        copy.wait_send()


def shards(hid, gain, segs, qc, qe, kc, ke, oc, oe):
    cosine, sine = rope_tables()
    kct = kc.transpose(1, 2, 0).reshape(128, FEAT)
    ket = ke.transpose(1, 2, 0).reshape(2, 16)
    hbm, vmem, smem = (pl.BlockSpec(memory_space=m) for m in (pl.ANY, pltpu.VMEM, pltpu.SMEM))
    types = len(TYPES)
    scratch = [
        ((FEAT, QC), BF16), ((FEAT, 128), BF16), ((QC, FEAT), BF16), ((128, FEAT), BF16),
        ((16, QC), F32), ((8, FEAT), F32), ((3, 128, HD), F32), ((3, 128, HD), F32),
        ((NC, 2, 2, 4, 16, FEAT), BF16), ((NC, 256, FEAT), BF16), ((256, 128), F32),
        ((8, 256), F32), ((7, 8, 256), F32), ((NC, 32, 128), F32),
        ((NC, UNITS, 2, 4, 32, QH), BF16), ((NC, UNITS, 2, 32, QH), BF16), ((NC, UNITS, 2, 32, QH), BF16),
        ((NC, UNITS, 2, 2, 32, QH), BF16), ((NC, UNITS, 32, QH), BF16), ((NC, 32, QC), F32),
        ((2, 4, 2, 4, 16, 128), BF16), ((7, 2, 4, 16, 128), BF16), ((3, 2, 2, 4, 16, 128), BF16),
        ((384, 128), BF16), ((384, 128), BF16), ((256, 128), BF16),
        ((NC, 2, 4, 2, 16, QC), BF16), ((NC, UNITS, 2, 2, 4, 16, OH), BF16), ((NC, UNITS, 2, 4, 16, OH), BF16),
        ((NC, UNITS, 2, 4, 16, OH), BF16), ((NC, UNITS, 2, 16, OH), BF16), ((NC, UNITS, 2, 16, OH), BF16),
        ((NC, UNITS, 2, 2, 16, OH), BF16), ((NC, UNITS, 16, OH), BF16),
    ]
    scratch = [pltpu.VMEM(shape, dtype) for shape, dtype in scratch]
    dma = pltpu.SemaphoreType.DMA
    scratch += [dma((types, NC * UNITS)), dma((types, NC * UNITS))]
    scratch += [dma((7,)), dma((7,)), dma((7,)), dma((7,)), dma((5,)), dma((5,)), dma((13,))]
    return pl.pallas_call(
        layer,
        out_shape=jax.ShapeDtypeStruct((64, FEAT), BF16),
        in_specs=[hbm, vmem, vmem, hbm, vmem, hbm, smem, hbm, vmem, hbm, hbm],
        out_specs=vmem,
        scratch_shapes=scratch,
        compiler_params=pltpu.CompilerParams(collective_id=0, has_side_effects=True, vmem_limit_bytes=60 * 1024 * 1024),
        name="layer",
    )(hid, gain.reshape(1, FEAT), segs.reshape(8, 128), qc, qe, kct, ket, oc, oe, jnp.asarray(cosine), jnp.asarray(sine))


def solution(mesh):
    placed = (
        P(("gy", "gz"), "gx"),
        P("gx"),
        P(),
        P("gx", ("gy", "gz")),
        P("gx", ("gy", "gz")),
        P("gx", None, ("gy", "gz")),
        P("gx", None, ("gy", "gz")),
        P(("gy", "gz"), "gx"),
        P(("gy", "gz"), "gx"),
    )
    return jax.shard_map(shards, mesh=mesh, in_specs=placed, out_specs=P(("gy", "gz"), "gx"), check_vma=False)
```

time: 120 us -> 99.4 us (0.83)
  Pallas kernels: 116 us -> 96.3 us
    pallas_call x1, Pallas kernels: 116 us -> 96.3 us  [shards(): pl.pallas_call(layer, out_shape=jax.ShapeDtypeStruct((64, FEAT), BF16), i...]
where the time goes in v2:
time: 99.4 us; the launch traced here: 99.2 us
  Pallas kernels  96.3 us (97%)
  local copies, waits for them, and re-layouts  2.96 us (3%)
    pallas_call x1, Pallas kernels, shards(): pl.pallas_call(layer, out_shape=jax.ShapeDtypeStruct((64, FEAT), BF16), i...  96.3 us

profile of v2, /device:TPU:1, one launch (start us, length us, event | category | flops | bytes accessed | tf_op | source)
XLA Modules:
  0.0 99.2 jit_solution(903404592992281058)
XLA Ops:
  0.0 1.3 %reshape.12.gain = bf16[1,2048]{1,0:T(2,128)(2,1)} reshape(bf16[2048]{0:T(1024)(128)(2,1)} %param.12) | data formatting | bytes 8192 | tf_op jit(solution)/shard_map/reshape | solution.py:478
  1.3 96.3 %layer.1 = bf16[64,2048]{1,0:T(8,128)(2,1)} custom-call(bf16[64,2048]{1,0:T(8,128)(2,1)} %hid.1, bf16[1,2048]{1,0:T(2,128)(2,1)} %reshape.12.gain, s32[8,128]{1,0:T(8,128)} %bitcast.8, bf16[2048,1024]{1,0:T(8,128)(2,1)} %qc.1, s32[16,16]{1,0:T(8,128)} %qe.1, bf16[128,2048]{1,0:T(8,128)(2,1)} %bitcast.7, s32[2,16]{1,0:T(2,128)} %bitcast.9, ...), custom_call_target="tpu_custom_call" | custom-call | tf_op jit(solution)/shard_map/layer/pallas_call | solution.py:470
  97.6 1.7 %copy.13 = bf16[64,2048]{1,0:T(8,128)(2,1)} copy(bf16[64,2048]{1,0:T(8,128)(2,1)} %layer.1) | data formatting | bytes 524288

commit v3 on v2

v3 whole, which is shorter than its diff:
```python
import math

import jax
import jax.numpy as jnp
import numpy as np
from jax import lax
from jax.experimental import pallas as pl
from jax.experimental.pallas import tpu as pltpu
from jax.sharding import PartitionSpec as P

D = 16384
HD = 128
TOKENS = 1024
THETA = 500000.0
EPS = 1e-05
NC = 4
FEAT = 2048
QC = 1024
QH, OH = 512, 1024
F32, BF16 = jnp.float32, jnp.bfloat16
MESH = pl.DeviceIdType.MESH

UNITS = 2
RECV = {"a_x": NC, "a_p": NC, "a_m": NC, "a_r": NC, "a_s": NC, "b_2": NC * UNITS, "b_3": NC * UNITS, "sums": 1, "kvp": 1}
RECV.update({"kv": 1, "c_x": NC, "c_p": NC, "c_m": NC, "c_r": NC, "d_s": NC * UNITS, "d_2": NC * UNITS, "d_3": NC * UNITS})
SEND = ["a_x", "a_z", "a_s", "b_2", "b_3", "sums", "kvp", "kv", "c_x", "c_y", "d_s", "d_2", "d_3"]
SEND = {name: i for i, name in enumerate(SEND)}

ORDER = (
    ("A0", 0), ("A0", 1), ("A1", 0), ("A0", 2), ("A1", 1), ("A2", 0), ("A1", 2), ("DQ", 0), ("A2", 1), ("A0", 3),
    ("A3", 0), ("HG", 0), ("A1", 3), ("MM", 0), ("A3", 1), ("A2", 2), ("MM", 1), ("HG", 1), ("A2", 3), ("B2", 0),
    ("MM", 11), ("A3", 2), ("MM", 10), ("B2", 1), ("HG", 2), ("A3", 3), ("B2", 11), ("MM", 20), ("HG", 3),
    ("KS", 0), ("DO", 0), ("B2", 10), ("MM", 21), ("B4", 0), ("B2", 20), ("KX", 0), ("MM", 31), ("MM", 30),
    ("B4", 10), ("B4", 1), ("B2", 21), ("KY", 0), ("B2", 31), ("AT", 0), ("B4", 11), ("AT", 1), ("B2", 30),
    ("B4", 20), ("C1", 0), ("B4", 21), ("C1", 1), ("AT", 2), ("C2", 0), ("C2", 1), ("B4", 31), ("B4", 30),
    ("C1", 2), ("AT", 3), ("C3", 0), ("MO", 1), ("C3", 1), ("MO", 11), ("D1", 1), ("C2", 2), ("MO", 10), ("C1", 3),
    ("D1", 11), ("MO", 0), ("D2", 1), ("D1", 10), ("C3", 2), ("MO", 20), ("D2", 11), ("C2", 3), ("D1", 0),
    ("MO", 21), ("D4", 1), ("D1", 20), ("D1", 21), ("D2", 10), ("C3", 3), ("D2", 0), ("MO", 31), ("MO", 30),
    ("D1", 31), ("D1", 30), ("D2", 20), ("D2", 21), ("D2", 31), ("D2", 30), ("D4", 0), ("D4", 21), ("D4", 10),
    ("D4", 20), ("D4", 11), ("D4", 31), ("D4", 30),
)


def rope_tables():
    frequency = np.exp(np.arange(HD // 2, dtype=np.float64) * (-2.0 * math.log(THETA) / HD))
    angles = np.arange(TOKENS, dtype=np.float64)[:, None] * frequency[None, :]
    cosine, sine = np.cos(angles), np.sin(angles)
    cosine = np.concatenate([cosine, cosine], axis=1).astype(np.float32)
    sine = np.concatenate([-sine, sine], axis=1).astype(np.float32)
    return np.stack([cosine.reshape(8, 128, HD), sine.reshape(8, 128, HD)], axis=1)


def layer(
    hid, gain, segs, qc, qe, kc, ke, oc, oe, rope_hbm, out,
    wq, wk, wo, kct, scale_q, scale_o, rope,
    g, x, squares, sums, sums_in, factors,
    qp, b2, bu, b3, qown,
    kvp, kv_in, kv, kb, vb, qr,
    ag, pp, d_in, dt, d2, du, d3,
    send_sem, recv_sem, local,
):
    gx, gy, gz = lax.axis_index("gx"), lax.axis_index("gy"), lax.axis_index("gz")
    xlo, y, xhi, core, z = gx // 4, gx % 4, gy // 2, gy % 2, gz
    yp, ym, y2 = (y + 1) % 4, (y + 3) % 4, (y + 2) % 4
    zp, zm, z2 = (z + 1) % 4, (z + 3) % 4, (z + 2) % 4
    oxlo, oxhi, ocore = 1 - xlo, 1 - xhi, 1 - core
    odd = z % 2
    zo = z + 1 - 2 * odd
    dev_s = (gx, xhi * 2 + ocore, gz)
    dev_xhi = (gx, oxhi * 2 + core, gz)
    dev_zp, dev_zm = (gx, gy, zp), (gx, gy, zm)
    dev_xlo = (oxlo * 4 + y, gy, gz)
    dev_yp, dev_ym = (xlo * 4 + yp, gy, gz), (xlo * 4 + ym, gy, gz)
    peers = [(a, b) for a in range(2) for b in range(4) if (a, b) != (0, 0)]
    dev_peers = [(((xlo + a) % 2) * 4 + (y + b) % 4, gy, gz) for a, b in peers]
    dev_kv = [(1, (gx, gy, zo))]
    for d in (1, 2):
        dev_kv += [(2 * d, ((gx + d) % 8, gy, z)), (2 * d + 1, ((gx + d) % 8, gy, zo))]

    copies = {}

    def fetch(name, index, src, dst):
        copies[name] = pltpu.make_async_copy(src, dst, local.at[index])
        copies[name].start()

    fetch("hid", 0, hid, g.at[:, xhi, core, z])
    fetch("kc", 1, kc, kct)
    fetch("qc", 2, qc, wq)
    for d in range(3):
        pltpu.make_async_copy(rope_hbm.at[(gx + 8 - d) % 8], rope.at[d], local.at[3]).start()
    fetch("oc", 4, oc, wo)

    barrier = pltpu.get_barrier_semaphore()
    greeted = [dev_s, dev_xhi, dev_zp, dev_zm, (gx, oxhi * 2 + core, zp), (gx, oxhi * 2 + core, zm)] + dev_peers
    greeted += [((gx + d) % 8, gy, zo) for d in (1, 2, 6, 7)]
    for other in greeted:
        pl.semaphore_signal(barrier, inc=1, device_id=other, device_id_type=MESH)
    pl.semaphore_wait(barrier, len(greeted))

    first_sem, total = {}, 0
    for name, count in RECV.items():
        first_sem[name] = total
        total += count

    def send(name, i, src, dst, to, group=None):
        pltpu.make_async_remote_copy(
            src_ref=src, dst_ref=dst, send_sem=send_sem.at[SEND[group or name]], recv_sem=recv_sem.at[first_sem[name] + i],
            device_id=to, device_id_type=MESH,
        ).start()

    def came(name, i, dst):
        pltpu.make_async_remote_copy(
            src_ref=dst, dst_ref=dst, send_sem=send_sem.at[0], recv_sem=recv_sem.at[first_sem[name] + i],
            device_id=dev_s, device_id_type=MESH,
        ).wait_recv()

    def left(group, src):
        pltpu.make_async_remote_copy(
            src_ref=src, dst_ref=src, send_sem=send_sem.at[SEND[group]], recv_sem=recv_sem.at[0],
            device_id=dev_s, device_id_type=MESH,
        ).wait_send()

    def step_a0(c):
        if c == 0:
            copies["hid"].wait()
        own = g.at[c, xhi, core, z]
        send("a_x", c, own, own, dev_xhi)
        send("a_p", c, own, own, dev_zp, "a_z")
        send("a_m", c, own, own, dev_zm, "a_z")
        send("a_s", c, own, own, dev_s)

    def step_a1(c):
        block = g.at[c, oxhi, core, z]
        came("a_x", c, block)
        send("a_p", c, block, block, dev_zp, "a_z")
        send("a_m", c, block, block, dev_zm, "a_z")
        send("a_s", c, block, block, dev_s)

    def step_a2(c):
        both = g.at[c, :, core, zm]
        came("a_p", c, both)
        relay = g.at[c, 0, core, zm]
        send("a_r", c, relay, relay, dev_zp, "a_z")
        send("a_s", c, both, both, dev_s)
        both = g.at[c, :, core, zp]
        came("a_m", c, both)
        relay = g.at[c, 1, core, zp]
        send("a_r", c, relay, relay, dev_zm, "a_z")
        send("a_s", c, both, both, dev_s)

    def step_a3(c):
        both = g.at[c, :, core, z2]
        came("a_r", c, both)
        send("a_s", c, both, both, dev_s)

    def step_dq(_):
        rows = lax.broadcasted_iota(jnp.int32, (16, QC), 0)
        cols = lax.broadcasted_iota(jnp.int32, (16, QC), 1)
        spread = jnp.where(rows == cols // 64, 1.0, 0.0).astype(BF16)
        powers = jnp.exp2(qe[...].astype(F32)).astype(BF16)
        scale_q[...] = jnp.dot(powers, spread, preferred_element_type=F32) * (1.0 / 128.0)
        copies["kc"].wait()
        lane = lax.broadcasted_iota(jnp.int32, (1, 128), 1)

        def key_block(k, carry):
            at = pl.multiple_of(k * 128, 128)
            e = jnp.where(lane < 64, ke[0, k], ke[1, k]).astype(F32)
            scale = jnp.exp2(e) * (1.0 / 128.0)
            block = kct[:, pl.ds(at, 128)].astype(F32).T
            wk[pl.ds(at, 128), :] = (block * scale).astype(BF16)
            return carry

        lax.fori_loop(0, 16, key_block, 0)
        copies["qc"].wait()

        def query_block(k, carry):
            at = pl.multiple_of(k * 128, 128)
            scale = scale_q[pl.ds(k, 1), :]
            wq[pl.ds(at, 128), :] = (wq[pl.ds(at, 128), :].astype(F32) * scale).astype(BF16)
            return carry

        lax.fori_loop(0, 16, query_block, 0)
        sums[...] = jnp.zeros_like(sums)

    def step_do(_):
        rows = lax.broadcasted_iota(jnp.int32, (32, FEAT), 0)
        cols = lax.broadcasted_iota(jnp.int32, (32, FEAT), 1)
        spread = jnp.where(rows == cols // 64, 1.0, 0.0).astype(BF16)
        powers = jnp.exp2(oe[...].astype(F32)).astype(BF16)
        scale_o[...] = jnp.dot(powers, spread, preferred_element_type=F32) * (1.0 / 128.0)
        copies["oc"].wait()

        def output_block(k, carry):
            at = pl.multiple_of(k * 128, 128)
            scale = scale_o[pl.ds(k, 1), :]
            wo[pl.ds(at, 128), :] = (wo[pl.ds(at, 128), :].astype(F32) * scale).astype(BF16)
            return carry

        lax.fori_loop(0, 8, output_block, 0)

    def step_hg(c):
        came("a_s", c, g.at[c, :, ocore])
        weight = jnp.concatenate([gain[k:k + 1, :] for k in range(FEAT // 128)], axis=1).astype(F32)

        def scaled(p, carry):
            block = g[c, p // 8, (p // 4) % 2, p % 4].astype(F32)
            at = pl.multiple_of(p * 16, 16)
            x[c, pl.ds(at, 16), :] = (block * weight).astype(BF16)
            total = block[:, :128] * block[:, :128]
            for k in range(1, FEAT // 128):
                piece = block[:, k * 128:(k + 1) * 128]
                total = total + piece * piece
            squares[pl.ds(at, 16), :] = total
            return carry

        lax.fori_loop(0, 16, scaled, 0)
        sums[c:c + 1, :] = jnp.sum(squares[...].T, axis=0, keepdims=True)
        part = jnp.dot(x[c], wk[...], preferred_element_type=F32)
        kvp[:, :, :, c] = part.astype(BF16).reshape(2, 4, 2, 16, 128)

    def step_mm(k):
        c, u = k // 10, k % 10
        i = c * UNITS + u

        def columns(n, carry):
            at = pl.multiple_of(n * 256, 256)
            part = jnp.dot(x[c], wq[:, pl.ds(u * QH + at, 256)], preferred_element_type=F32)
            qp[c, u, :, :, :, pl.ds(at, 256)] = part.astype(BF16).reshape(2, 4, 32, 256)
            return carry

        lax.fori_loop(0, QH // 256, columns, 0)
        send("b_2", i, qp.at[c, u, 0, y2], b2.at[c, u, 0], dev_yp)
        send("b_2", i, qp.at[c, u, 1, y2], b2.at[c, u, 1], dev_ym)
        send("b_3", i, qp.at[c, u, 1, yp], b3.at[c, u, 2 - xlo], (4 + yp, gy, gz))
        send("b_3", i, qp.at[c, u, 0, ym], b3.at[c, u, 3 + xlo], (ym, gy, gz))
        send("b_3", i, qp.at[c, u, oxlo, y], b3.at[c, u, 0], dev_xlo)

    def step_b2(k):
        c, u = k // 10, k % 10
        i = c * UNITS + u
        came("b_2", i, b2.at[c, u])
        bu[c, u, 0] = qp[c, u, 0, yp] + b2[c, u, 0]
        send("b_3", i, bu.at[c, u, 0], b3.at[c, u, 1 + xlo], (yp, gy, gz))
        bu[c, u, 1] = qp[c, u, 1, ym] + b2[c, u, 1]
        send("b_3", i, bu.at[c, u, 1], b3.at[c, u, 4 - xlo], (4 + ym, gy, gz))

    def step_b4(k):
        c, u = k // 10, k % 10
        came("b_3", c * UNITS + u, b3.at[c, u])
        total = qp[c, u, xlo, y].astype(F32)
        for slot in range(5):
            total = total + b3[c, u, slot].astype(F32)
        qown[c, :, u * QH:(u + 1) * QH] = total

    def step_ks(_):
        for i, to in enumerate(dev_peers):
            a, b = peers[i]
            send("sums", 0, sums, sums_in.at[i], to)
            send("kvp", 0, kvp.at[(xlo + a) % 2, (y + b) % 4], kv_in.at[i], to)

    def rows_of(table, c):
        return jnp.concatenate([table[c * 16:c * 16 + 16], table[64 + c * 16:64 + c * 16 + 16]], axis=0)

    def rotated(field, cosine, sine):
        return field * cosine + pltpu.roll(field, 64, 1) * sine

    def step_kx(_):
        came("sums", 0, sums_in)
        total = sums[...]
        for i in range(len(peers)):
            total = total + sums_in[i]
        inverse = lax.rsqrt(total * (1.0 / D) + EPS)
        lane = lax.broadcasted_iota(jnp.int32, (32, 256), 1)
        row = lax.broadcasted_iota(jnp.int32, (32, 256), 0)
        for c in range(NC):
            spread = jnp.where(lane == row + 32 * gx, inverse[c:c + 1, :], 0.0)
            factors[c] = jnp.broadcast_to(jnp.sum(spread, axis=1, keepdims=True), (32, 128))
        came("kvp", 0, kv_in)
        for c in range(NC):
            part = kvp[xlo, y, :, c].astype(F32)
            for i in range(len(peers)):
                part = part + kv_in[i, :, c].astype(F32)
            kv[0, :, c] = (part.reshape(32, 128) * factors[c]).astype(BF16).reshape(2, 16, 128)
        for place, to in dev_kv:
            send("kv", 0, kv.at[0], kv.at[place], to)

    def step_ky(_):
        pltpu.make_async_copy(rope, rope, local.at[3]).wait()
        came("kv", 0, kv.at[pl.ds(1, 5)])
        low = lax.broadcasted_iota(jnp.int32, (128, 128), 1) < 64
        for d in range(3):
            at = (2 - d) * 128
            first = kv[2 * d + odd].reshape(128, 128).astype(F32)
            second = kv[2 * d + 1 - odd].reshape(128, 128).astype(F32)
            keys = jnp.where(low, first, pltpu.roll(second, 64, 1))
            kb[at:at + 128, :] = rotated(keys, rope[d, 0], rope[d, 1]).astype(BF16)
            vb[at:at + 128, :] = jnp.where(low, pltpu.roll(first, 64, 1), second).astype(BF16)

    def step_at(c):
        cosine, sine = rows_of(rope[0, 0], c), rows_of(rope[0, 1], c)
        factor = factors[c]
        for h in range(8):
            head = qown[c, :, h * 128:(h + 1) * 128] * factor
            qr[h * 32:(h + 1) * 32, :] = rotated(head, cosine, sine).astype(BF16)
        row = lax.broadcasted_iota(jnp.int32, (32, 128), 0)
        lane = lax.broadcasted_iota(jnp.int32, (32, 128), 1)
        mine = segs[pl.ds(gx, 1), :].astype(F32)
        token = (row // 16) * 64 + c * 16 + row % 16
        query_segments = jnp.sum(jnp.where(lane == token, mine, 0.0), axis=1, keepdims=True)
        key_segments = jnp.concatenate([segs[pl.ds((gx + 8 - d) % 8, 1), :] for d in (2, 1, 0)], axis=1).astype(F32)
        row = lax.broadcasted_iota(jnp.int32, (32, 384), 0)
        place = lax.broadcasted_iota(jnp.int32, (32, 384), 1)
        token = (row // 16) * 64 + c * 16 + row % 16
        allowed = (query_segments == key_segments) & (place <= token + 256) & (place >= 256 - 128 * gx)
        masked = jnp.where(allowed, 0.0, -jnp.inf)
        scores = lax.dot_general(qr[...], kb[...], (((1,), (1,)), ((), ())), preferred_element_type=F32)
        scores = (scores * (1.0 / math.sqrt(HD))).reshape(8, 32, 384) + masked[None]
        weights = jnp.exp(scores - jnp.max(scores, axis=2, keepdims=True))
        weights = (weights / jnp.sum(weights, axis=2, keepdims=True)).astype(BF16).reshape(256, 384)
        heads = jnp.dot(weights, vb[...], preferred_element_type=F32).astype(BF16)
        for h in range(8):
            ag[c, xlo, y, :, :, h * 128:(h + 1) * 128] = heads[h * 32:(h + 1) * 32].reshape(2, 16, 128)
        own = ag.at[c, xlo, y]
        send("c_x", c, own, own, dev_xlo)
        send("c_p", c, own, own, dev_yp, "c_y")
        send("c_m", c, own, own, dev_ym, "c_y")

    def step_c1(c):
        block = ag.at[c, oxlo, y]
        came("c_x", c, block)
        send("c_p", c, block, block, dev_yp, "c_y")
        send("c_m", c, block, block, dev_ym, "c_y")

    def step_c2(c):
        came("c_p", c, ag.at[c, :, ym])
        relay = ag.at[c, 0, ym]
        send("c_r", c, relay, relay, dev_yp, "c_y")
        came("c_m", c, ag.at[c, :, yp])
        relay = ag.at[c, 1, yp]
        send("c_r", c, relay, relay, dev_ym, "c_y")

    def step_c3(c):
        came("c_r", c, ag.at[c, :, y2])

    def step_mo(k):
        c, u = k // 10, k % 10
        i = c * UNITS + u
        rows = ag[c].reshape(256, QC)

        def columns(n, carry):
            at = pl.multiple_of(n * 256, 256)
            part = jnp.dot(rows, wo[:, pl.ds(u * OH + at, 256)], preferred_element_type=F32)
            pp[c, u, :, :, :, :, pl.ds(at, 256)] = part.astype(BF16).reshape(2, 2, 4, 16, 256)
            return carry

        lax.fori_loop(0, OH // 256, columns, 0)
        send("d_s", i, pp.at[c, u, :, ocore], d_in.at[c, u], dev_s)

    def step_d1(k):
        c, u = k // 10, k % 10
        i = c * UNITS + u
        came("d_s", i, d_in.at[c, u])

        def add(w):
            for h in range(2):
                dt[c, u, h, w] = pp[c, u, h, core, w] + d_in[c, u, h, w]

        add(z2)
        send("d_2", i, dt.at[c, u, 0, z2], d2.at[c, u, 0], dev_zp)
        send("d_2", i, dt.at[c, u, 1, z2], d2.at[c, u, 1], dev_zm)
        add(zp)
        send("d_3", i, dt.at[c, u, 1, zp], d3.at[c, u, 2 - xhi], (gx, 2 + core, zp))
        add(zm)
        send("d_3", i, dt.at[c, u, 0, zm], d3.at[c, u, 3 + xhi], (gx, core, zm))
        add(z)
        send("d_3", i, dt.at[c, u, oxhi, z], d3.at[c, u, 0], dev_xhi)

    def step_d2(k):
        c, u = k // 10, k % 10
        i = c * UNITS + u
        came("d_2", i, d2.at[c, u])
        du[c, u, 0] = dt[c, u, 0, zp] + d2[c, u, 0]
        send("d_3", i, du.at[c, u, 0], d3.at[c, u, 1 + xhi], (gx, core, zp))
        du[c, u, 1] = dt[c, u, 1, zm] + d2[c, u, 1]
        send("d_3", i, du.at[c, u, 1], d3.at[c, u, 4 - xhi], (gx, 2 + core, zm))

    def step_d4(k):
        c, u = k // 10, k % 10
        came("d_3", c * UNITS + u, d3.at[c, u])
        columns = slice(u * OH, (u + 1) * OH)
        total = g[c, xhi, core, z, :, columns].astype(F32) + dt[c, u, xhi, z].astype(F32)
        for slot in range(5):
            total = total + d3[c, u, slot].astype(F32)
        out[16 * c:16 * c + 16, columns] = total.astype(BF16)

    table = {
        "A0": step_a0, "A1": step_a1, "A2": step_a2, "A3": step_a3, "DQ": step_dq, "DO": step_do, "HG": step_hg,
        "MM": step_mm, "B2": step_b2, "B4": step_b4, "KS": step_ks, "KX": step_kx, "KY": step_ky, "AT": step_at,
        "C1": step_c1, "C2": step_c2, "C3": step_c3, "MO": step_mo, "D1": step_d1, "D2": step_d2, "D4": step_d4,
    }
    for name, c in ORDER:
        table[name](c)
    sources = {
        "a_x": g.at[:, 0, 0, 0], "a_z": g.at[pl.ds(0, 3), 0], "a_s": g.at[:, :, 0], "b_2": b2, "b_3": b3,
        "sums": sums_in, "kvp": kv_in, "kv": kv.at[pl.ds(1, 5)], "c_x": ag.at[:, 0, 0], "c_y": ag.at[pl.ds(0, 3)],
        "d_s": d_in, "d_2": d2, "d_3": d3,
    }
    for group, source in sources.items():
        left(group, source)


def shards(hid, gain, segs, qc, qe, kc, ke, oc, oe):
    rope = jnp.asarray(rope_tables())
    kct = kc.transpose(1, 2, 0).reshape(128, FEAT)
    ket = ke.transpose(1, 2, 0).reshape(2, 16)
    hbm, vmem, smem = (pl.BlockSpec(memory_space=m) for m in (pl.ANY, pltpu.VMEM, pltpu.SMEM))
    scratch = [
        ((FEAT, QC), BF16), ((FEAT, 128), BF16), ((QC, FEAT), BF16), ((128, FEAT), BF16),
        ((16, QC), F32), ((8, FEAT), F32), ((3, 2, 128, HD), F32),
        ((NC, 2, 2, 4, 16, FEAT), BF16), ((NC, 256, FEAT), BF16), ((256, 128), F32),
        ((8, 256), F32), ((7, 8, 256), F32), ((NC, 32, 128), F32),
        ((NC, UNITS, 2, 4, 32, QH), BF16), ((NC, UNITS, 2, 32, QH), BF16), ((NC, UNITS, 2, 32, QH), BF16),
        ((NC, UNITS, 5, 32, QH), BF16), ((NC, 32, QC), F32),
        ((2, 4, 2, 4, 16, 128), BF16), ((7, 2, 4, 16, 128), BF16), ((6, 2, 4, 16, 128), BF16),
        ((384, 128), BF16), ((384, 128), BF16), ((256, 128), BF16),
        ((NC, 2, 4, 2, 16, QC), BF16), ((NC, UNITS, 2, 2, 4, 16, OH), BF16), ((NC, UNITS, 2, 4, 16, OH), BF16),
        ((NC, UNITS, 2, 4, 16, OH), BF16), ((NC, UNITS, 2, 16, OH), BF16), ((NC, UNITS, 2, 16, OH), BF16),
        ((NC, UNITS, 5, 16, OH), BF16),
    ]
    scratch = [pltpu.VMEM(shape, dtype) for shape, dtype in scratch]
    dma = pltpu.SemaphoreType.DMA
    scratch += [dma((len(SEND),)), dma((sum(RECV.values()),)), dma((5,))]
    return pl.pallas_call(
        layer,
        out_shape=jax.ShapeDtypeStruct((64, FEAT), BF16),
        in_specs=[hbm, vmem, vmem, hbm, vmem, hbm, smem, hbm, vmem, hbm],
        out_specs=vmem,
        scratch_shapes=scratch,
        compiler_params=pltpu.CompilerParams(collective_id=0, has_side_effects=True, vmem_limit_bytes=60 * 1024 * 1024),
        name="layer",
    )(hid.reshape(NC, 16, FEAT), gain.reshape(16, 128), segs.reshape(8, 128), qc, qe, kct, ket, oc, oe, rope)


def solution(mesh):
    placed = (
        P(("gy", "gz"), "gx"),
        P("gx"),
        P(),
        P("gx", ("gy", "gz")),
        P("gx", ("gy", "gz")),
        P("gx", None, ("gy", "gz")),
        P("gx", None, ("gy", "gz")),
        P(("gy", "gz"), "gx"),
        P(("gy", "gz"), "gx"),
    )
    return jax.shard_map(shards, mesh=mesh, in_specs=placed, out_specs=P(("gy", "gz"), "gx"), check_vma=False)
```

time: 99.4 us -> 93.7 us (0.943)
  Pallas kernels: 96.3 us -> 91.9 us
  local copies, waits for them, and re-layouts: 2.96 us -> 1.67 us
    pallas_call x1, Pallas kernels: 96.3 us -> 91.9 us  [shards(): pl.pallas_call(layer, out_shape=jax.ShapeDtypeStruct((64, FEAT), BF16), i...]
    reshape x1 -> x0, local copies, waits for them, and re-layouts: 1.29 us -> none  [shards(): gain.reshape(1, FEAT)]
where the time goes in v3:
time: 93.7 us; the launch traced here: 93.6 us
  Pallas kernels  91.9 us (98%)
  local copies, waits for them, and re-layouts  1.67 us (2%)
    pallas_call x1, Pallas kernels, shards(): pl.pallas_call(layer, out_shape=jax.ShapeDtypeStruct((64, FEAT), BF16), i...  91.9 us

profile of v3, /device:TPU:1, one launch (start us, length us, event | category | flops | bytes accessed | tf_op | source)
XLA Modules:
  0.0 93.6 jit_solution(10618558107387750125)
XLA Ops:
  0.0 91.9 %layer.1 = bf16[64,2048]{1,0:T(8,128)(2,1)} custom-call(bf16[4,16,2048]{2,1,0:T(8,128)(2,1)} %bitcast.10, bf16[16,128]{1,0:T(8,128)(2,1)} %bitcast.11, s32[8,128]{1,0:T(8,128)} %bitcast.12, bf16[2048,1024]{1,0:T(8,128)(2,1)} %qc.1, s32[16,16]{1,0:T(8,128)} %qe.1, bf16[128,2048]{1,0:T(8,128)(2,1)} %bitcast.9, s32[2,16]{1,0:T(2,128)} %bitcast.13, ...), custom_call_target="tpu_custom_call" | custom-call | tf_op jit(solution)/shard_map/layer/pallas_call | solution.py:433
  91.9 1.7 %copy.12 = bf16[64,2048]{1,0:T(8,128)(2,1)} copy(bf16[64,2048]{1,0:T(8,128)(2,1)} %layer.1) | data formatting | bytes 524288

commit v4 on v3

v4 whole, which is shorter than its diff:
```python
import math

import jax
import jax.numpy as jnp
import numpy as np
from jax import lax
from jax.experimental import pallas as pl
from jax.experimental.pallas import tpu as pltpu
from jax.sharding import PartitionSpec as P

D = 16384
HD = 128
TOKENS = 1024
THETA = 500000.0
EPS = 1e-05
NC = 4
FEAT = 2048
QC = 1024
QH, OH = 512, 1024
F32, BF16 = jnp.float32, jnp.bfloat16
MESH = pl.DeviceIdType.MESH

UNITS = 2
GATHER_A = "b0b0"
GATHER_C = "bb00"
SPLIT_A = "1111"
SPLIT_C = "1111"
SUM_B = "yyyyxgyy"
SUM_D = "ggyyxyyg"
GATHER_COPIES = ("x", "p", "m", "pc", "mc", "r")


def semaphore_names():
    names = []
    for c in range(NC):
        names += [("a_s", c), ("kvp", c)]
        for letter, modes, split in (("a_", GATHER_A, SPLIT_A), ("c_", GATHER_C, SPLIT_C)):
            for k in range(c * 10, c * 10 + int(split[c])):
                names += [(letter + kind, k) for kind in GATHER_COPIES + (("x2",) if modes[c] == "b" else ())]
        for i in (2 * c, 2 * c + 1):
            names += [("d_s", i)]
            for letter, modes in (("b_", SUM_B), ("d_", SUM_D)):
                names += [(letter + kind, i) for kind in ("2", "3") + (("x",) if modes[i] != "g" else ())]
    return names + [("sums", 0), ("sums", 1), ("kv", 0), ("kv", 1)]


RECV = {name: i for i, name in enumerate(semaphore_names())}
SEND = ["a0", "a1", "a_s", "b0", "b1", "sums", "kvp", "kv", "c0", "c1", "d_s", "d0", "d1"]
SEND = {name: i for i, name in enumerate(SEND)}

ORDER = (
    ("A0", 0), ("A0", 10), ("DQ", 0), ("A0", 20), ("A1", 0), ("A1", 10), ("A0", 30), ("A2", 0), ("A1", 30),
    ("A2", 10), ("A3", 0), ("A1", 20), ("HG", 0), ("MM", 1), ("A3", 10), ("A2", 30), ("A2", 20), ("MM", 0),
    ("HG", 1), ("B2", 1), ("MM", 10), ("A3", 30), ("B2", 0), ("A3", 20), ("MM", 11), ("HG", 2), ("B2", 10),
    ("HG", 3), ("MM", 20), ("B2", 11), ("MM", 31), ("B3", 1), ("KX", 0), ("B3", 10), ("KX", 1), ("B3", 11),
    ("MM", 21), ("B1", 20), ("B3", 0), ("MM", 30), ("B2", 31), ("B4", 1), ("KY", 0), ("B2", 21), ("B4", 10),
    ("B4", 11), ("AT", 1), ("C0", 10), ("B2", 20), ("B4", 0), ("AT", 0), ("B2", 30), ("C0", 0), ("DO", 0),
    ("B3", 31), ("C1", 10), ("B4", 20), ("B4", 21), ("B3", 30), ("AT", 2), ("C0", 20), ("C2", 10), ("C1", 0),
    ("B4", 31), ("B4", 30), ("AT", 3), ("C0", 30), ("C1", 20), ("C2", 0), ("C3", 10), ("MO", 11), ("C1", 30),
    ("MO", 10), ("D0", 11), ("C2", 20), ("C3", 0), ("MO", 1), ("D0", 10), ("MO", 0), ("D0", 1), ("C2", 30),
    ("D2", 11), ("C3", 20), ("D0", 0), ("MO", 20), ("MO", 21), ("D2", 1), ("D2", 10), ("D0", 20), ("C3", 30),
    ("MO", 30), ("D0", 21), ("MO", 31), ("D3", 11), ("D0", 30), ("D3", 10), ("D0", 31), ("D2", 30), ("D2", 21),
    ("D4", 1), ("D1", 20), ("D4", 11), ("D2", 0), ("D2", 31), ("D3", 30), ("D3", 21), ("D2", 20), ("D4", 10),
    ("D4", 30), ("D4", 20), ("D4", 0), ("D4", 21), ("D4", 31),
)


START = [c for name, c in ORDER if name == "A0"][0]


def rope_tables():
    frequency = np.exp(np.arange(HD // 2, dtype=np.float64) * (-2.0 * math.log(THETA) / HD))
    angles = np.arange(TOKENS, dtype=np.float64)[:, None] * frequency[None, :]
    cosine, sine = np.cos(angles), np.sin(angles)
    cosine = np.concatenate([cosine, cosine], axis=1).astype(np.float32)
    sine = np.concatenate([-sine, sine], axis=1).astype(np.float32)
    return np.stack([cosine.reshape(8, 128, HD), sine.reshape(8, 128, HD)], axis=1)


def layer(
    hid, gain_hbm, segs_hbm, qc, qe_hbm, kc, ke_hbm, oc, oe_hbm, rope_hbm, out,
    gain, segs, qe, ke, oe,
    wq, wk, wo, kct, scale_q, scale_o, rope,
    g, x, squares, sums, sums_in, factors,
    qp, b2, bu, b3, bx, qown,
    kvp, kv_in, kv, kb, vb, qr,
    ag, pp, d_in, dt, d2, du, d3, dx,
    send_sem, recv_sem, local,
):
    gx, gy, gz = lax.axis_index("gx"), lax.axis_index("gy"), lax.axis_index("gz")
    xlo, y, xhi, core, z = gx // 4, gx % 4, gy // 2, gy % 2, gz
    yp, ym, y2 = (y + 1) % 4, (y + 3) % 4, (y + 2) % 4
    zp, zm, z2 = (z + 1) % 4, (z + 3) % 4, (z + 2) % 4
    oxlo, oxhi, ocore = 1 - xlo, 1 - xhi, 1 - core
    odd = z % 2
    zo = z + 1 - 2 * odd
    dev_s = (gx, xhi * 2 + ocore, gz)
    dev_xhi = (gx, oxhi * 2 + core, gz)
    dev_zp, dev_zm = (gx, gy, zp), (gx, gy, zm)
    dev_xlo = (oxlo * 4 + y, gy, gz)
    dev_yp, dev_ym = (xlo * 4 + yp, gy, gz), (xlo * 4 + ym, gy, gz)
    peers = [(a, b) for a in range(2) for b in range(4) if (a, b) != (0, 0)]
    dev_peers = [(((xlo + a) % 2) * 4 + (y + b) % 4, gy, gz) for a, b in peers]
    dev_kv = [(1, (gx, gy, zo))]
    for d in (1, 2):
        dev_kv += [(2 * d, ((gx + d) % 8, gy, z)), (2 * d + 1, ((gx + d) % 8, gy, zo))]

    barrier = pltpu.get_barrier_semaphore()
    greeted = [(gx, oxhi * 2 + core, (z + d) % 4) for d in (2, 1, 3, 0)] + [(gx, gy, (z + d) % 4) for d in (2, 1, 3)]
    greeted += [dev_s] + dev_peers
    greeted += [((gx + d) % 8, gy, zo) for d in (1, 2, 6, 7)]
    for other in greeted:
        pl.semaphore_signal(barrier, inc=1, device_id=other, device_id_type=MESH)

    copies = {}

    def fetch(name, index, src, dst):
        copies[name] = pltpu.make_async_copy(src, dst, local.at[index])
        copies[name].start()

    fetch("hid", 0, hid, g.at[:, xhi, core, z])
    fetch("ke", 5, ke_hbm, ke)
    fetch("qe", 6, qe_hbm, qe)
    fetch("kc", 1, kc, kct)
    fetch("qc", 2, qc, wq)
    for d in range(3):
        pltpu.make_async_copy(rope_hbm.at[(gx + 8 - d) % 8], rope.at[d], local.at[3]).start()
    fetch("gain", 7, gain_hbm, gain)
    fetch("segs", 8, segs_hbm, segs)
    fetch("oe", 9, oe_hbm, oe)
    fetch("oc", 4, oc, wo)

    pl.semaphore_wait(barrier, len(greeted))

    def send(name, i, src, dst, to, group):
        pltpu.make_async_remote_copy(
            src_ref=src, dst_ref=dst, send_sem=send_sem.at[SEND[group]], recv_sem=recv_sem.at[RECV[name, i]],
            device_id=to, device_id_type=MESH,
        ).start()

    def came(name, i, dst):
        pltpu.make_async_remote_copy(
            src_ref=dst, dst_ref=dst, send_sem=send_sem.at[0], recv_sem=recv_sem.at[RECV[name, i]],
            device_id=dev_s, device_id_type=MESH,
        ).wait_recv()

    def left(group, src):
        pltpu.make_async_remote_copy(
            src_ref=src, dst_ref=src, send_sem=send_sem.at[SEND[group]], recv_sem=recv_sem.at[0],
            device_id=dev_s, device_id_type=MESH,
        ).wait_send()

    def gather(letter, modes, split, blocks, width, h, w, device, neighbour):
        oh, wp, wm, w2 = 1 - h, (w + 1) % 4, (w + 3) % 4, (w + 2) % 4
        across, plus, minus = device(oh, w), device(h, wp), device(h, wm)

        def mode(k):
            return modes[k // 10]

        def buffer(k, column, at, piece=0, pieces=1):
            count = int(split[k // 10]) * pieces
            return blocks(k // 10, column, at, pl.ds((k % 10 * pieces + piece) * (width // count), width // count))

        def copy(kind, k, block, to):
            send(letter + "_" + kind, k, block, block, to, letter + str(k // 20))

        def await_block(kind, k, block):
            came(letter + "_" + kind, k, block)

        def first(k):
            own = buffer(k, h, w)
            copy("x", k, own, across)
            copy("p", k, own, plus)
            copy("m", k, own, minus)
            neighbour(k, own)
            if mode(k) == "D":
                copy("r", k, own, device(h, w2))
                copy("pc", k, own, device(oh, wp))
                copy("mc", k, own, device(oh, wm))
                copy("r", k, own, device(oh, w2))

        def second(k):
            if mode(k) == "b":
                await_block("p", k, buffer(k, h, wm))
                copy("r", k, buffer(k, h, wm, 0, 2), plus)
                neighbour(k, buffer(k, h, wm))
                await_block("m", k, buffer(k, h, wp))
                copy("r", k, buffer(k, h, wp, 1, 2), minus)
                neighbour(k, buffer(k, h, wp))
            block = buffer(k, oh, w)
            await_block("x", k, block)
            copy("pc", k, block, plus)
            copy("mc", k, block, minus)
            neighbour(k, block)

        def third(k):
            if mode(k) == "b":
                block = buffer(k, h, w2)
                await_block("r", k, block)
                copy("x2", k, block, across)
                neighbour(k, block)
                return
            await_block("p", k, buffer(k, h, wm))
            await_block("pc", k, buffer(k, oh, wm))
            copy("r", k, buffer(k, 0, wm), plus)
            await_block("m", k, buffer(k, h, wp))
            await_block("mc", k, buffer(k, oh, wp))
            copy("r", k, buffer(k, 1, wp), minus)
            neighbour(k, buffer(k, slice(None), wm))
            neighbour(k, buffer(k, slice(None), wp))

        def fourth(k):
            if mode(k) == "b":
                for kind, at in (("pc", wm), ("mc", wp), ("x2", w2)):
                    block = buffer(k, oh, at)
                    await_block(kind, k, block)
                    neighbour(k, block)
                return
            if mode(k) == "D":
                await_block("x", k, buffer(k, oh, w))
                neighbour(k, buffer(k, oh, w))
                for kind, at in (("p", wm), ("m", wp)):
                    await_block(kind, k, buffer(k, h, at))
                    await_block(kind + "c", k, buffer(k, oh, at))
                    neighbour(k, buffer(k, slice(None), at))
            both = buffer(k, slice(None), w2)
            await_block("r", k, both)
            neighbour(k, both)

        return first, second, third, fourth

    def scatter(letter, modes, part, r2, ru, r3, rx, width, h, w, device, finish):
        oh, wp, wm, w2 = 1 - h, (w + 1) % 4, (w + 3) % 4, (w + 2) % 4
        across, plus, minus = device(oh, w), device(h, wp), device(h, wm)
        low, high = pl.ds(0, width // 2), pl.ds(width // 2, width // 2)

        def copy(kind, k, src, dst, to):
            i = k // 10 * UNITS + k % 10
            send(letter + "_" + kind, i, src, dst, to, letter + str(k // 20))

        def await_blocks(kind, k, blocks):
            came(letter + "_" + kind, k // 10 * UNITS + k % 10, blocks)

        def mode(k):
            return modes[k // 10 * UNITS + k % 10]

        def begin(k):
            c, u = k // 10, k % 10
            if mode(k) == "x":
                copy("x", k, part.at[c, u, oh], rx.at[c, u], across)
                return
            copy("2", k, part.at[c, u, 0, w2], r2.at[c, u, 0], plus)
            copy("2", k, part.at[c, u, 1, w2], r2.at[c, u, 1], minus)
            if mode(k) == "g":
                copy("3", k, part.at[c, u, 1, wp], r3.at[c, u, 2 - h], device(1, wp))
                copy("3", k, part.at[c, u, 0, wm], r3.at[c, u, 3 + h], device(0, wm))
                copy("3", k, part.at[c, u, oh, w], r3.at[c, u, 0], across)
            else:
                copy("3", k, part.at[c, u, 1, wp], r3.at[c, u, 2], plus)
                copy("3", k, part.at[c, u, 0, wm], r3.at[c, u, 3], minus)

        def one(k):
            c, u = k // 10, k % 10
            await_blocks("x", k, rx.at[c, u])

            def add(at):
                part[c, u, h, at] = part[c, u, h, at] + rx[c, u, at]

            add(w2)
            copy("2", k, part.at[c, u, h, w2, :, low], r2.at[c, u, 0, :, low], plus)
            copy("2", k, part.at[c, u, h, w2, :, high], r2.at[c, u, 1, :, high], minus)
            add(wp)
            copy("3", k, part.at[c, u, h, wp, :, high], r3.at[c, u, 1, :, high], plus)
            add(wm)
            copy("3", k, part.at[c, u, h, wm, :, low], r3.at[c, u, 3, :, low], minus)
            add(w)

        def two(k):
            c, u = k // 10, k % 10
            if mode(k) == "x":
                await_blocks("2", k, r2.at[c, u, 0])
                ru[c, u, 0, :, low] = part[c, u, h, wp, :, low] + r2[c, u, 0, :, low]
                copy("3", k, ru.at[c, u, 0, :, low], r3.at[c, u, 1, :, low], plus)
                ru[c, u, 1, :, high] = part[c, u, h, wm, :, high] + r2[c, u, 1, :, high]
                copy("3", k, ru.at[c, u, 1, :, high], r3.at[c, u, 3, :, high], minus)
                return
            await_blocks("2", k, r2.at[c, u])
            ru[c, u, 0] = part[c, u, 0, wp] + r2[c, u, 0]
            if mode(k) == "g":
                copy("3", k, ru.at[c, u, 0], r3.at[c, u, 1 + h], device(0, wp))
            else:
                copy("3", k, ru.at[c, u, 0], r3.at[c, u, 1], plus)
            ru[c, u, 1] = part[c, u, 1, wm] + r2[c, u, 1]
            if mode(k) == "g":
                copy("3", k, ru.at[c, u, 1], r3.at[c, u, 4 - h], device(1, wm))
            else:
                copy("3", k, ru.at[c, u, 1], r3.at[c, u, 4], minus)

        def three(k):
            c, u = k // 10, k % 10
            await_blocks("3", k, r3.at[c, u, pl.ds(1, 4)])
            total = part[c, u, oh, w].astype(F32) + r3[c, u, 1 + oh].astype(F32) + r3[c, u, 3 + oh].astype(F32)
            part[c, u, oh, w] = total.astype(BF16)
            copy("x", k, part.at[c, u, oh, w], r3.at[c, u, 0], across)

        def four(k):
            c, u = k // 10, k % 10
            total = part[c, u, h, w].astype(F32)
            if mode(k) == "g":
                await_blocks("3", k, r3.at[c, u])
                slots = range(5)
            elif mode(k) == "y":
                await_blocks("x", k, r3.at[c, u, 0])
                slots = (0, 1 + h, 3 + h)
            else:
                await_blocks("3", k, r3.at[c, u, pl.ds(1, 2)])
                slots = (1, 3)
            for slot in slots:
                total = total + r3[c, u, slot].astype(F32)
            finish(c, u, total)

        return begin, one, two, three, four

    def to_core(k, block):
        send("a_s", k // 10, block, block, dev_s, "a_s")

    gather_a = gather(
        "a", GATHER_A, SPLIT_A, lambda c, h, w, some: g.at[c, h, core, w, :, some], FEAT,
        xhi, z, lambda h, w: (gx, h * 2 + core, w), to_core,
    )

    def step_dq(_):
        rows = lax.broadcasted_iota(jnp.int32, (16, QC), 0)
        cols = lax.broadcasted_iota(jnp.int32, (16, QC), 1)
        spread = jnp.where(rows == cols // 64, 1.0, 0.0).astype(BF16)
        copies["qe"].wait()
        copies["ke"].wait()
        copies["gain"].wait()
        powers = jnp.exp2(qe[...].astype(F32)).astype(BF16)
        scale_q[...] = jnp.dot(powers, spread, preferred_element_type=F32) * (1.0 / 128.0)
        copies["kc"].wait()
        lane = lax.broadcasted_iota(jnp.int32, (1, 128), 1)

        def key_block(k, carry):
            at = pl.multiple_of(k * 128, 128)
            e = jnp.where(lane < 64, ke[0, k], ke[1, k]).astype(F32)
            scale = jnp.exp2(e) * (1.0 / 128.0)
            block = kct[:, pl.ds(at, 128)].astype(F32).T
            wk[pl.ds(at, 128), :] = (block * scale).astype(BF16)
            return carry

        lax.fori_loop(0, 16, key_block, 0)
        copies["qc"].wait()

        def query_block(k, carry):
            at = pl.multiple_of(k * 128, 128)
            scale = scale_q[pl.ds(k, 1), :]
            wq[pl.ds(at, 128), :] = (wq[pl.ds(at, 128), :].astype(F32) * scale).astype(BF16)
            return carry

        lax.fori_loop(0, 16, query_block, 0)
        sums[...] = jnp.zeros_like(sums)

    def step_do(_):
        rows = lax.broadcasted_iota(jnp.int32, (32, FEAT), 0)
        cols = lax.broadcasted_iota(jnp.int32, (32, FEAT), 1)
        spread = jnp.where(rows == cols // 64, 1.0, 0.0).astype(BF16)
        copies["oe"].wait()
        powers = jnp.exp2(oe[...].astype(F32)).astype(BF16)
        scale_o[...] = jnp.dot(powers, spread, preferred_element_type=F32) * (1.0 / 128.0)
        copies["oc"].wait()

        def output_block(k, carry):
            at = pl.multiple_of(k * 128, 128)
            scale = scale_o[pl.ds(k, 1), :]
            wo[pl.ds(at, 128), :] = (wo[pl.ds(at, 128), :].astype(F32) * scale).astype(BF16)
            return carry

        lax.fori_loop(0, 8, output_block, 0)

    def step_hg(c):
        came("a_s", c, g.at[c, :, ocore])
        weight = jnp.concatenate([gain[k:k + 1, :] for k in range(FEAT // 128)], axis=1).astype(F32)

        def scaled(p, carry):
            block = g[c, p // 8, (p // 4) % 2, p % 4].astype(F32)
            at = pl.multiple_of(p * 16, 16)
            x[c, pl.ds(at, 16), :] = (block * weight).astype(BF16)
            total = block[:, :128] * block[:, :128]
            for k in range(1, FEAT // 128):
                piece = block[:, k * 128:(k + 1) * 128]
                total = total + piece * piece
            squares[pl.ds(at, 16), :] = total
            return carry

        lax.fori_loop(0, 16, scaled, 0)
        sums[c // 3, c % 3:c % 3 + 1, :] = jnp.sum(squares[...].T, axis=0, keepdims=True)
        part = jnp.dot(x[c], wk[...], preferred_element_type=F32)
        kvp[c] = part.astype(BF16).reshape(2, 4, 2, 16, 128)
        for i, to in enumerate(dev_peers):
            a, b = peers[i]
            send("kvp", c, kvp.at[c, (xlo + a) % 2, (y + b) % 4], kv_in.at[c, i], to, "kvp")
            if c >= 2:
                send("sums", c - 2, sums.at[c - 2], sums_in.at[c - 2, i], to, "sums")

    def step_mm(k):
        c, u = k // 10, k % 10

        part = jnp.dot(x[c], wq[:, u * QH:(u + 1) * QH], preferred_element_type=F32)
        qp[c, u] = part.astype(BF16).reshape(2, 4, 32, QH)
        scatter_b[0](k)

    def keep_queries(c, u, total):
        qown[c, :, u * QH:(u + 1) * QH] = total

    scatter_b = scatter(
        "b", SUM_B, qp, b2, bu, b3, bx, QH, xlo, y, lambda h, w: (h * 4 + w, gy, gz), keep_queries,
    )

    def rows_of(table, c):
        return jnp.concatenate([table[c * 16:c * 16 + 16], table[64 + c * 16:64 + c * 16 + 16]], axis=0)

    def rotated(field, cosine, sine):
        return field * cosine + pltpu.roll(field, 64, 1) * sine

    def step_kx(part):
        came("sums", part, sums_in.at[part])
        total = sums[part]
        for i in range(len(peers)):
            total = total + sums_in[part, i]
        inverse = lax.rsqrt(total * (1.0 / D) + EPS)
        lane = lax.broadcasted_iota(jnp.int32, (32, 256), 1)
        row = lax.broadcasted_iota(jnp.int32, (32, 256), 0)
        chunks = range(3) if part == 0 else range(3, NC)
        for c in chunks:
            spread = jnp.where(lane == row + 32 * gx, inverse[c % 3:c % 3 + 1, :], 0.0)
            factors[c] = jnp.broadcast_to(jnp.sum(spread, axis=1, keepdims=True), (32, 128))
            came("kvp", c, kv_in.at[c])
            total = kvp[c, xlo, y].astype(F32)
            for i in range(len(peers)):
                total = total + kv_in[c, i].astype(F32)
            kv[0, c] = (total.reshape(32, 128) * factors[c]).astype(BF16).reshape(2, 16, 128)
        some = pl.ds(0, 3) if part == 0 else pl.ds(3, 1)
        for place, to in dev_kv:
            send("kv", part, kv.at[0, some], kv.at[place, some], to, "kv")

    def step_ky(_):
        pltpu.make_async_copy(rope, rope, local.at[3]).wait()
        copies["segs"].wait()
        came("kv", 0, kv.at[pl.ds(1, 5), pl.ds(0, 3)])
        came("kv", 1, kv.at[pl.ds(1, 5), pl.ds(3, 1)])

        def in_order(place):
            blocks = [kv[place, c, half] for half in range(2) for c in range(NC)]
            return jnp.concatenate(blocks, axis=0).astype(F32)

        low = lax.broadcasted_iota(jnp.int32, (128, 128), 1) < 64
        for d in range(3):
            at = (2 - d) * 128
            first = in_order(2 * d + odd)
            second = in_order(2 * d + 1 - odd)
            keys = jnp.where(low, first, pltpu.roll(second, 64, 1))
            kb[at:at + 128, :] = rotated(keys, rope[d, 0], rope[d, 1]).astype(BF16)
            vb[at:at + 128, :] = jnp.where(low, pltpu.roll(first, 64, 1), second).astype(BF16)

    def step_at(c):
        cosine, sine = rows_of(rope[0, 0], c), rows_of(rope[0, 1], c)
        factor = factors[c]
        for h in range(8):
            head = qown[c, :, h * 128:(h + 1) * 128] * factor
            qr[h * 32:(h + 1) * 32, :] = rotated(head, cosine, sine).astype(BF16)
        row = lax.broadcasted_iota(jnp.int32, (32, 128), 0)
        lane = lax.broadcasted_iota(jnp.int32, (32, 128), 1)
        mine = segs[pl.ds(gx, 1), :].astype(F32)
        token = (row // 16) * 64 + c * 16 + row % 16
        query_segments = jnp.sum(jnp.where(lane == token, mine, 0.0), axis=1, keepdims=True)
        key_segments = jnp.concatenate([segs[pl.ds((gx + 8 - d) % 8, 1), :] for d in (2, 1, 0)], axis=1).astype(F32)
        row = lax.broadcasted_iota(jnp.int32, (32, 384), 0)
        place = lax.broadcasted_iota(jnp.int32, (32, 384), 1)
        token = (row // 16) * 64 + c * 16 + row % 16
        allowed = (query_segments == key_segments) & (place <= token + 256) & (place >= 256 - 128 * gx)
        masked = jnp.where(allowed, 0.0, -jnp.inf)
        scores = lax.dot_general(qr[...], kb[...], (((1,), (1,)), ((), ())), preferred_element_type=F32)
        scores = (scores * (1.0 / math.sqrt(HD))).reshape(8, 32, 384) + masked[None]
        weights = jnp.exp(scores - jnp.max(scores, axis=2, keepdims=True))
        weights = (weights / jnp.sum(weights, axis=2, keepdims=True)).astype(BF16).reshape(256, 384)
        heads = jnp.dot(weights, vb[...], preferred_element_type=F32).astype(BF16)
        for h in range(8):
            ag[c, xlo, y, :, :, h * 128:(h + 1) * 128] = heads[h * 32:(h + 1) * 32].reshape(2, 16, 128)

    gather_c = gather(
        "c", GATHER_C, SPLIT_C, lambda c, h, w, some: ag.at[c, h, w, :, :, some], QC,
        xlo, y, lambda h, w: (h * 4 + w, gy, gz), lambda k, block: None,
    )

    def step_mo(k):
        c, u = k // 10, k % 10
        i = c * UNITS + u
        rows = ag[c].reshape(256, QC)

        part = jnp.dot(rows, wo[:, u * OH:(u + 1) * OH], preferred_element_type=F32)
        pp[c, u] = part.astype(BF16).reshape(2, 2, 4, 16, OH)
        send("d_s", i, pp.at[c, u, :, ocore], d_in.at[c, u], dev_s, "d_s")

    def step_d0(k):
        c, u = k // 10, k % 10
        came("d_s", c * UNITS + u, d_in.at[c, u])
        for h in range(2):
            for w in range(4):
                dt[c, u, h, w] = pp[c, u, h, core, w] + d_in[c, u, h, w]
        scatter_d[0](k)

    def keep_out(c, u, total):
        columns = slice(u * OH, (u + 1) * OH)
        out[16 * c:16 * c + 16, columns] = (g[c, xhi, core, z, :, columns].astype(F32) + total).astype(BF16)

    scatter_d = scatter(
        "d", SUM_D, dt, d2, du, d3, dx, OH, xhi, z, lambda h, w: (gx, h * 2 + core, w), keep_out,
    )

    table = {
        "DQ": step_dq, "DO": step_do, "HG": step_hg, "MM": step_mm, "KX": step_kx, "KY": step_ky, "AT": step_at,
        "MO": step_mo, "D0": step_d0,
    }
    table.update({"A%d" % i: step for i, step in enumerate(gather_a)})
    table.update({"C%d" % i: step for i, step in enumerate(gather_c)})
    table.update({"B%d" % i: step for i, step in enumerate(scatter_b) if i})
    table.update({"D%d" % i: step for i, step in enumerate(scatter_d) if i})
    for name, c in ORDER:
        if name == "A0" and c == START:
            copies["hid"].wait()
        table[name](c)
    sources = {
        "a_s": g.at[:, :, 0], "sums": sums_in, "kvp": kv_in, "kv": kv.at[pl.ds(1, 5)], "d_s": d_in,
    }
    for group in ("a0", "a1", "b0", "b1", "c0", "c1", "d0", "d1"):
        sources[group] = x.at[0, pl.ds(0, 224)]
    for group, source in sources.items():
        left(group, source)


def shards(hid, gain, segs, qc, qe, kc, ke, oc, oe):
    rope = jnp.asarray(rope_tables())
    kct = kc.transpose(1, 2, 0).reshape(128, FEAT)
    ket = ke.transpose(1, 2, 0).reshape(2, 16)
    hbm, vmem = pl.BlockSpec(memory_space=pl.ANY), pl.BlockSpec(memory_space=pltpu.VMEM)
    scratch = [
        ((FEAT, QC), BF16), ((FEAT, 128), BF16), ((QC, FEAT), BF16), ((128, FEAT), BF16),
        ((16, QC), F32), ((8, FEAT), F32), ((3, 2, 128, HD), F32),
        ((NC, 2, 2, 4, 16, FEAT), BF16), ((NC, 256, FEAT), BF16), ((256, 128), F32),
        ((2, 8, 256), F32), ((2, 7, 8, 256), F32), ((NC, 32, 128), F32),
        ((NC, UNITS, 2, 4, 32, QH), BF16), ((NC, UNITS, 2, 32, QH), BF16), ((NC, UNITS, 2, 32, QH), BF16),
        ((NC, UNITS, 5, 32, QH), BF16), ((NC, UNITS, 4, 32, QH), BF16), ((NC, 32, QC), F32),
        ((NC, 2, 4, 2, 16, 128), BF16), ((NC, 7, 2, 16, 128), BF16), ((6, NC, 2, 16, 128), BF16),
        ((384, 128), BF16), ((384, 128), BF16), ((256, 128), BF16),
        ((NC, 2, 4, 2, 16, QC), BF16), ((NC, UNITS, 2, 2, 4, 16, OH), BF16), ((NC, UNITS, 2, 4, 16, OH), BF16),
        ((NC, UNITS, 2, 4, 16, OH), BF16), ((NC, UNITS, 2, 16, OH), BF16), ((NC, UNITS, 2, 16, OH), BF16),
        ((NC, UNITS, 5, 16, OH), BF16), ((NC, UNITS, 4, 16, OH), BF16),
    ]
    small = [pltpu.VMEM((16, 128), BF16), pltpu.VMEM((8, 128), jnp.int32), pltpu.VMEM((16, 16), jnp.int32)]
    small += [pltpu.SMEM((2, 16), jnp.int32), pltpu.VMEM((8, 32), jnp.int32)]
    scratch = small + [pltpu.VMEM(shape, dtype) for shape, dtype in scratch]
    dma = pltpu.SemaphoreType.DMA
    scratch += [dma((len(SEND),)), dma((len(RECV),)), dma((10,))]
    return pl.pallas_call(
        layer,
        out_shape=jax.ShapeDtypeStruct((64, FEAT), BF16),
        in_specs=[hbm] * 10,
        out_specs=vmem,
        scratch_shapes=scratch,
        compiler_params=pltpu.CompilerParams(collective_id=0, has_side_effects=True, vmem_limit_bytes=60 * 1024 * 1024),
        name="layer",
    )(hid.reshape(NC, 16, FEAT), gain.reshape(16, 128), segs.reshape(8, 128), qc, qe, kct, ket, oc, oe, rope)


def solution(mesh):
    placed = (
        P(("gy", "gz"), "gx"),
        P("gx"),
        P(),
        P("gx", ("gy", "gz")),
        P("gx", ("gy", "gz")),
        P("gx", None, ("gy", "gz")),
        P("gx", None, ("gy", "gz")),
        P(("gy", "gz"), "gx"),
        P(("gy", "gz"), "gx"),
    )
    return jax.shard_map(shards, mesh=mesh, in_specs=placed, out_specs=P(("gy", "gz"), "gx"), check_vma=False)
```

time: 93.7 us -> 84.3 us (0.90)
  Pallas kernels: 91.9 us -> 82.4 us
    pallas_call x1, Pallas kernels: 91.9 us -> 82.4 us  [shards(): pl.pallas_call(layer, out_shape=jax.ShapeDtypeStruct((64, FEAT), BF16), i...]
where the time goes in v4:
time: 84.3 us; the launch traced here: 84.1 us
  Pallas kernels  82.4 us (98%)
  local copies, waits for them, and re-layouts  1.67 us (2%)
    pallas_call x1, Pallas kernels, shards(): pl.pallas_call(layer, out_shape=jax.ShapeDtypeStruct((64, FEAT), BF16), i...  82.4 us

profile of v4, /device:TPU:1, one launch (start us, length us, event | category | flops | bytes accessed | tf_op | source)
XLA Modules:
  0.0 84.1 jit_solution(1678246227613567638)
XLA Ops:
  0.0 82.4 %layer.1 = bf16[64,2048]{1,0:T(8,128)(2,1)} custom-call(bf16[4,16,2048]{2,1,0:T(8,128)(2,1)} %bitcast.10, bf16[16,128]{1,0:T(8,128)(2,1)} %bitcast.11, s32[8,128]{1,0:T(8,128)} %bitcast.12, bf16[2048,1024]{1,0:T(8,128)(2,1)} %qc.1, s32[16,16]{1,0:T(8,128)} %qe_hbm.1, bf16[128,2048]{1,0:T(8,128)(2,1)} %bitcast.9, s32[2,16]{1,0:T(2,128)} %bitcast.13, ...), custom_call_target="tpu_custom_call" | custom-call | tf_op jit(solution)/shard_map/layer/pallas_call | solution.py:565
  82.5 1.7 %copy.12 = bf16[64,2048]{1,0:T(8,128)(2,1)} copy(bf16[64,2048]{1,0:T(8,128)(2,1)} %layer.1) | data formatting | bytes 524288

commit v5 on v4

--- a/solution.py
+++ b/solution.py
@@ -49,12 +49,12 @@
 SEND = {name: i for i, name in enumerate(SEND)}
 
 ORDER = (
-    ("A0", 0), ("A0", 10), ("DQ", 0), ("A0", 20), ("A1", 0), ("A1", 10), ("A0", 30), ("A2", 0), ("A1", 30),
+    ("A0", 0), ("A0", 10), ("DQ", 0), ("A0", 20), ("A1", 0), ("A1", 10), ("A0", 30), ("A2", 0), ("DO", 0), ("A1", 30),
     ("A2", 10), ("A3", 0), ("A1", 20), ("HG", 0), ("MM", 1), ("A3", 10), ("A2", 30), ("A2", 20), ("MM", 0),
     ("HG", 1), ("B2", 1), ("MM", 10), ("A3", 30), ("B2", 0), ("A3", 20), ("MM", 11), ("HG", 2), ("B2", 10),
     ("HG", 3), ("MM", 20), ("B2", 11), ("MM", 31), ("B3", 1), ("KX", 0), ("B3", 10), ("KX", 1), ("B3", 11),
     ("MM", 21), ("B1", 20), ("B3", 0), ("MM", 30), ("B2", 31), ("B4", 1), ("KY", 0), ("B2", 21), ("B4", 10),
-    ("B4", 11), ("AT", 1), ("C0", 10), ("B2", 20), ("B4", 0), ("AT", 0), ("B2", 30), ("C0", 0), ("DO", 0),
+    ("B4", 11), ("AT", 1), ("C0", 10), ("B2", 20), ("B4", 0), ("AT", 0), ("B2", 30), ("C0", 0),
     ("B3", 31), ("C1", 10), ("B4", 20), ("B4", 21), ("B3", 30), ("AT", 2), ("C0", 20), ("C2", 10), ("C1", 0),
     ("B4", 31), ("B4", 30), ("AT", 3), ("C0", 30), ("C1", 20), ("C2", 0), ("C3", 10), ("MO", 11), ("C1", 30),
     ("MO", 10), ("D0", 11), ("C2", 20), ("C3", 0), ("MO", 1), ("D0", 10), ("MO", 0), ("D0", 1), ("C2", 30),
@@ -79,7 +79,7 @@
 
 def layer(
     hid, gain_hbm, segs_hbm, qc, qe_hbm, kc, ke_hbm, oc, oe_hbm, rope_hbm, out,
-    gain, segs, qe, ke, oe,
+    gain, segs, qe, ke, oe, result,
     wq, wk, wo, kct, scale_q, scale_o, rope,
     g, x, squares, sums, sums_in, factors,
     qp, b2, bu, b3, bx, qown,
@@ -106,7 +106,7 @@
         dev_kv += [(2 * d, ((gx + d) % 8, gy, z)), (2 * d + 1, ((gx + d) % 8, gy, zo))]
 
     barrier = pltpu.get_barrier_semaphore()
-    greeted = [(gx, oxhi * 2 + core, (z + d) % 4) for d in (2, 1, 3, 0)] + [(gx, gy, (z + d) % 4) for d in (2, 1, 3)]
+    greeted = [(gx, oxhi * 2 + core, (z + d) % 4) for d in (1, 3, 0)] + [(gx, gy, (z + d) % 4) for d in (1, 3)]
     greeted += [dev_s] + dev_peers
     greeted += [((gx + d) % 8, gy, zo) for d in (1, 2, 6, 7)]
     for other in greeted:
@@ -512,7 +512,9 @@
 
     def keep_out(c, u, total):
         columns = slice(u * OH, (u + 1) * OH)
-        out[16 * c:16 * c + 16, columns] = (g[c, xhi, core, z, :, columns].astype(F32) + total).astype(BF16)
+        result[16 * c:16 * c + 16, columns] = (g[c, xhi, core, z, :, columns].astype(F32) + total).astype(BF16)
+        block = (pl.ds(16 * c, 16), pl.ds(u * OH, OH))
+        fetch("out%d" % (c * UNITS + u), 10 + c * UNITS + u, result.at[block], out.at[block])
 
     scatter_d = scatter(
         "d", SUM_D, dt, d2, du, d3, dx, OH, xhi, z, lambda h, w: (gx, h * 2 + core, w), keep_out,
@@ -530,6 +532,8 @@
         if name == "A0" and c == START:
             copies["hid"].wait()
         table[name](c)
+    for i in range(NC * UNITS):
+        copies["out%d" % i].wait()
     sources = {
         "a_s": g.at[:, :, 0], "sums": sums_in, "kvp": kv_in, "kv": kv.at[pl.ds(1, 5)], "d_s": d_in,
     }
@@ -543,7 +547,7 @@
     rope = jnp.asarray(rope_tables())
     kct = kc.transpose(1, 2, 0).reshape(128, FEAT)
     ket = ke.transpose(1, 2, 0).reshape(2, 16)
-    hbm, vmem = pl.BlockSpec(memory_space=pl.ANY), pl.BlockSpec(memory_space=pltpu.VMEM)
+    hbm = pl.BlockSpec(memory_space=pl.ANY)
     scratch = [
         ((FEAT, QC), BF16), ((FEAT, 128), BF16), ((QC, FEAT), BF16), ((128, FEAT), BF16),
         ((16, QC), F32), ((8, FEAT), F32), ((3, 2, 128, HD), F32),
@@ -558,15 +562,15 @@
         ((NC, UNITS, 5, 16, OH), BF16), ((NC, UNITS, 4, 16, OH), BF16),
     ]
     small = [pltpu.VMEM((16, 128), BF16), pltpu.VMEM((8, 128), jnp.int32), pltpu.VMEM((16, 16), jnp.int32)]
-    small += [pltpu.SMEM((2, 16), jnp.int32), pltpu.VMEM((8, 32), jnp.int32)]
+    small += [pltpu.SMEM((2, 16), jnp.int32), pltpu.VMEM((8, 32), jnp.int32), pltpu.VMEM((64, FEAT), BF16)]
     scratch = small + [pltpu.VMEM(shape, dtype) for shape, dtype in scratch]
     dma = pltpu.SemaphoreType.DMA
-    scratch += [dma((len(SEND),)), dma((len(RECV),)), dma((10,))]
+    scratch += [dma((len(SEND),)), dma((len(RECV),)), dma((10 + NC * UNITS,))]
     return pl.pallas_call(
         layer,
         out_shape=jax.ShapeDtypeStruct((64, FEAT), BF16),
         in_specs=[hbm] * 10,
-        out_specs=vmem,
+        out_specs=hbm,
         scratch_shapes=scratch,
         compiler_params=pltpu.CompilerParams(collective_id=0, has_side_effects=True, vmem_limit_bytes=60 * 1024 * 1024),
         name="layer",

time: 84.3 us -> 84.2 us (level)
  no operation moved by 1% of the time
where the time goes in v5:
time: 84.2 us; the launch traced here: 84.1 us
  Pallas kernels  82.4 us (98%)
  local copies, waits for them, and re-layouts  1.67 us (2%)
    pallas_call x1, Pallas kernels, shards(): pl.pallas_call(layer, out_shape=jax.ShapeDtypeStruct((64, FEAT), BF16), i...  82.4 us

profile of v5, /device:TPU:1, one launch (start us, length us, event | category | flops | bytes accessed | tf_op | source)
XLA Modules:
  0.0 84.1 jit_solution(2589288923814670056)
XLA Ops:
  0.0 82.4 %layer.1 = bf16[64,2048]{1,0:T(8,128)(2,1)} custom-call(bf16[4,16,2048]{2,1,0:T(8,128)(2,1)} %bitcast.10, bf16[16,128]{1,0:T(8,128)(2,1)} %bitcast.11, s32[8,128]{1,0:T(8,128)} %bitcast.12, bf16[2048,1024]{1,0:T(8,128)(2,1)} %qc.1, s32[16,16]{1,0:T(8,128)} %qe_hbm.1, bf16[128,2048]{1,0:T(8,128)(2,1)} %bitcast.9, s32[2,16]{1,0:T(2,128)} %bitcast.13, ...), custom_call_target="tpu_custom_call" | custom-call | tf_op jit(solution)/shard_map/layer/pallas_call | solution.py:569
  82.4 1.7 %copy.12 = bf16[64,2048]{1,0:T(8,128)(2,1)} copy(bf16[64,2048]{1,0:T(8,128)(2,1)} %layer.1) | data formatting | bytes 524288
